TPU v7x, 128 devices: a whole 4x4x4 slice. The times are simulated.
128 devices in a mesh: rows: 64 (over x_lo, y, z, core), sub: 2 (over x_hi).
Axes of the slice: x: 4 (x_hi: 2, x_lo: 2; x = x_hi * 2 + x_lo), y: 4, z: 4, core: 2. Of those that a mesh axis runs over, the one named last changes fastest.
Arguments:
- vectors: bfloat16 [131072, 1024], P(('rows', 'sub')), may hold values from -10 to 10
- list_ids: int32 [131072], P(('rows', 'sub')), may hold values from 0 to 65535, as said below
- codes: int32 [131072, 64], P(('rows', 'sub')), may hold values from 0 to 255
- centroids: bfloat16 [65536, 1024], P(('rows', 'sub')), may hold values from -6 to 6
- codebooks: float32 [64, 16, 256], P('sub'), may hold values from -6 to 6
Outputs:
- new_centroids: float32 [65536, 1024], P(('rows', 'sub'))
- new_codebooks: float32 [64, 16, 256], P('sub')
- distortion: float32 [64, 256], P('sub')
Inputs may be any that keep to these rules, and one draw needn't show every extreme that they name: `list_ids`: in each device's block of 1024 rows, the j-th run of 8 rows holds only ids from j * 512 to j * 512 + 511.
All inputs are finite; a program needn't handle non-finite values.
Results may differ from a plain program's by a relative error of at most 0.0003.
Values may be sent and summed in bfloat16 or wider, within the bound.
No kernel may reach another device: no remote copies, remote signals or barrier semaphores. Data moves between devices by JAX's collectives and lax.ppermute only.
A program may use at most 192 MiB of HBM per device.

v0:
```python
import math

import jax
import jax.numpy as jnp
from jax import lax
from jax.sharding import PartitionSpec as P


def first_pass(resid_half, code_half, levels):
    total_rows, columns = resid_half.shape
    half_subs = code_half.shape[1]
    sub_width = columns // half_subs
    block_rows = math.gcd(total_rows, 512)
    blocks = total_rows // block_rows
    resid_blocks = resid_half.reshape(blocks, block_rows, half_subs, sub_width)
    code_blocks = code_half.reshape(blocks, block_rows, half_subs)
    count_levels = levels.shape[0]

    def first_add_block(running, pieces):
        totals, tallies, squares = running
        portion, portion_codes = pieces
        onehot = (jnp.transpose(portion_codes)[:, None, :] == levels[None, :, None]).astype(
            jnp.bfloat16
        )
        totals = totals + jnp.einsum(
            "mkr,rmd->mdk", onehot, portion, preferred_element_type=jnp.float32
        )
        tallies = tallies + jnp.sum(onehot, axis=2, dtype=jnp.float32)
        return ((totals, tallies, squares), None)

    start = (
        jnp.zeros((half_subs, sub_width, count_levels), jnp.float32),
        jnp.zeros((half_subs, count_levels), jnp.float32),
        jnp.zeros((half_subs, count_levels), jnp.float32),
    )
    result, _unused = lax.scan(first_add_block, start, (resid_blocks, code_blocks))
    return result


def error_pass(resid_half, code_half, levels, table):
    total_rows, columns = resid_half.shape
    half_subs = code_half.shape[1]
    sub_width = columns // half_subs
    block_rows = math.gcd(total_rows, 512)
    blocks = total_rows // block_rows
    resid_blocks = resid_half.reshape(blocks, block_rows, half_subs, sub_width)
    code_blocks = code_half.reshape(blocks, block_rows, half_subs)

    def error_add_block(running, pieces):
        portion, portion_codes = pieces
        onehot = (jnp.transpose(portion_codes)[:, None, :] == levels[None, :, None]).astype(
            jnp.float32
        )
        selected = jnp.einsum("mkr,mdk->rmd", onehot, table, precision=lax.Precision.HIGHEST)
        gap = portion.astype(jnp.float32) - selected
        gap_norms = jnp.sum(gap * gap, axis=2)
        return (
            running + jnp.einsum("mkr,rm->mk", onehot, gap_norms, precision=lax.Precision.HIGHEST),
            None,
        )

    start = jnp.zeros((half_subs, levels.shape[0]), jnp.float32)
    errors, _unused = lax.scan(error_add_block, start, (resid_blocks, code_blocks))
    return errors


def on_device(vectors, list_ids, codes, centroids, codebooks):
    rows_dev, model_dims = vectors.shape
    owners_rows = lax.axis_size("rows")
    owners_sub = lax.axis_size("sub")
    owners = owners_rows * owners_sub
    list_dev = centroids.shape[0]
    local_ids = list_ids % list_dev
    arrived, arrived_ids, arrived_codes = (
        lax.all_to_all(vectors, ("rows", "sub"), split_axis=0, concat_axis=0, tiled=True),
        lax.all_to_all(local_ids, ("rows", "sub"), split_axis=0, concat_axis=0, tiled=True),
        lax.all_to_all(codes, ("rows", "sub"), split_axis=0, concat_axis=0, tiled=True),
    )
    list_levels = jnp.arange(list_dev, dtype=jnp.int32)
    onehot = (list_levels[:, None] == arrived_ids[None, :]).astype(jnp.bfloat16)
    list_totals = jnp.dot(onehot, arrived, preferred_element_type=jnp.float32)
    list_counts = jnp.sum(onehot, axis=1, dtype=jnp.float32)
    prior_lists = rows_dev // list_dev
    new_centroids = (list_totals + prior_lists * centroids.astype(jnp.float32)) / (
        list_counts[:, None] + prior_lists
    )
    residual = (arrived.astype(jnp.float32) - jnp.take(new_centroids, arrived_ids, axis=0)).astype(
        jnp.bfloat16
    )
    count_levels = codebooks.shape[2]
    code_levels = jnp.arange(count_levels, dtype=jnp.int32)
    prior_codes = rows_dev * owners // count_levels
    resid_half, code_half = (
        lax.all_to_all(residual, "sub", split_axis=1, concat_axis=0, tiled=True),
        lax.all_to_all(arrived_codes, "sub", split_axis=1, concat_axis=0, tiled=True),
    )
    totals, tallies, _unused = first_pass(resid_half, code_half, code_levels)
    totals, tallies = lax.psum((totals, tallies), "rows")
    table = (totals + prior_codes * codebooks) / (tallies[:, None, :] + prior_codes)
    errors = lax.psum(error_pass(resid_half, code_half, code_levels, table), "rows")
    distortion = errors / (tallies + 1.0)
    return (new_centroids, table, distortion)


def solution(mesh):
    in_specs = (
        P(("rows", "sub"), None),
        P(("rows", "sub")),
        P(("rows", "sub"), None),
        P(("rows", "sub"), None),
        P("sub", None, None),
    )
    out_specs = (P(("rows", "sub"), None), P("sub", None, None), P("sub", None))
    return jax.shard_map(
        on_device, mesh=mesh, in_specs=in_specs, out_specs=out_specs, check_vma=False
    )
```

profile of v0, /device:TPU:1, one launch (start us, length us, event | category | flops | bytes accessed | tf_op | source)
XLA Modules:
  0.0 1056.9 jit_solution(6187491760942308666)
XLA Ops:
  7.2 0.7 add_select_fusion
  7.9 0.7 all_to_all.44
  8.6 11.5 %all-to-all-start = ((s32[128,8,1]{1,2,0:T(1,128)}), s32[128,8,1]{1,2,0:T(1,128)S(1)}, u32[]{:S(2)}, u32[]{:S(2)}) async-start(s32[128,8,1]{1,2,0:T(1,128)} %bitcast), calls=%async_computation | async-start | bytes 131072 | tf_op jit(solution)/shard_map/all_to_all | solution.py:76
  20.1 1.1 copy.33
  21.2 0.3 reshape.112
  21.6 8.1 all-to-all-done
  29.6 15.1 %all_to_all.62 = s32[128,1,512]{2,1,0:T(1,128)S(1)} all-to-all(s32[128,1,512]{2,1,0:T(1,128)S(1)} %reshape.112), channel_id=1, replica_groups=mesh['rows'=64,'sub'=2] {'rows','sub'}, dimensions={0} | all-to-all | bytes 524288 | tf_op jit(solution)/shard_map/all_to_all | solution.py:77
  44.7 4.5 all-to-all-start.1
  49.2 0.5 broadcast.81
  49.8 0.8 reduce.5
  50.6 0.1 eq.44
  50.7 0.1 all_to_all.49
  50.8 0.3 convert_reduce_fusion.1
  51.1 0.5 broadcast.82
  51.6 1.3 reduce.6
  52.9 0.9 reshape.113
  53.8 1.6 all_to_all.54
  55.5 1.1 copy.34
  56.6 22.3 %all-to-all-done.1 = bf16[128,8,1024]{2,1,0:T(8,128)(2,1)S(1)} async-done(((bf16[128,8,1024]{2,1,0:T(8,128)(2,1)}), bf16[128,8,1024]{2,1,0:T(8,128)(2,1)S(1)}, u32[]{:S(2)}, u32[]{:S(2)}) %all-to-all-start.1) | async-done | bytes 2097184 | tf_op jit(solution)/shard_map/all_to_all | solution.py:75
  78.9 1.4 copy-done.1
  80.2 3.4 all-to-all-start.4
  83.7 3.1 add_divide_fusion
  86.8 0.0 copy-start
  86.8 5.4 gather_fusion
  92.3 6.6 gather.7
  98.9 6.6 reshape.88
  105.4 6.4 subtract_convert_fusion
  111.8 1.7 copy.31
  113.5 0.0 all-to-all-done.4
  113.5 4.2 all-to-all-start.2
  117.8 0.2 copy.35
  118.0 0.3 reshape.86
  118.2 0.1 copy.37
  118.3 23.7 %all-to-all-done.2 = bf16[1024,2,512]{2,0,1:T(8,128)(2,1)S(1)} async-done(((bf16[1024,2,512]{2,0,1:T(8,128)(2,1)}), bf16[1024,2,512]{2,0,1:T(8,128)(2,1)S(1)}, u32[]{:S(2)}, u32[]{:S(2)}) %all-to-all-start.2) | async-done | bytes 2097184 | tf_op jit(solution)/shard_map/all_to_all | solution.py:94
  142.0 4.1 copy.32
  146.1 5.3 reshape.85
  151.3 1.8 copy.36
  153.2 22.1 %while.24 = (s32[]{:T(128)}, f32[32,16,256]{2,1,0:T(8,128)S(1)}, f32[32,256]{1,0:T(8,128)S(1)}, bf16[4,512,32,16]{1,3,2,0:T(8,128)(2,1)}, s32[4,512,32]{1,2,0:T(8,128)S(1)}, /*index=5*/s32[]{:T(128)}, s32[]{:T(128)}) while((s32[]{:T(128)}, f32[32,16,256]{2,1,0:T(8,128)S(1)}, f32[32,256]{1,0:T(8,128)S(1)}, ...), condition=%wide.region_3.4_spmd.clone, body=%wide.region_1.3_spmd.clone.sunk | while | flops 155459584 | bytes 1966684 | solution.py:36
  153.2 3.7 fusion.35
  156.9 1.8 convert_reduce_fusion.3
  158.8 3.7 fusion.35
  162.5 1.8 convert_reduce_fusion.3
  164.3 3.7 fusion.35
  168.0 1.8 convert_reduce_fusion.3
  169.8 3.7 fusion.35
  173.5 1.8 convert_reduce_fusion.3
  175.3 0.0 copy-start.4
  175.3 0.8 copy-done.4
  176.1 0.0 all-reduce.2.cloned.1.call-update
  176.1 271.8 %psum.22 = f32[32,256]{1,0:T(8,128)S(1)} all-reduce(f32[32,256]{1,0:T(8,128)S(1)} %get-tuple-element.69), channel_id=1, replica_groups=mesh['rows'=64,'sub'=2] {'rows'}, use_global_device_ids=true, to_apply=%region_5.6 | all-reduce | flops 8192 | bytes 65536 | tf_op jit(solution)/shard_map/psum | solution.py:98
  447.9 269.9 %all-reduce.2.cloned.1.call-done = f32[32,16,256]{2,1,0:T(8,128)} async-done(((f32[32,16,256]{2,1,0:T(8,128)}), f32[32,16,256]{2,1,0:T(8,128)}) %all-reduce.2.cloned.1.call-update) | async-done | bytes 524304 | tf_op jit(solution)/shard_map/psum | solution.py:98
  717.8 1.2 add_divide_fusion.1
  719.0 55.6 %while.25 = (s32[]{:T(128)}, f32[32,256]{1,0:T(8,128)S(1)}, s32[4,512,32]{1,2,0:T(8,128)S(1)}, bf16[4,512,32,16]{1,3,2,0:T(8,128)(2,1)}, f32[32,16,256]{2,1,0:T(8,128)S(1)}, /*index=5*/s32[]{:T(128)}, s32[]{:T(128)}) while((s32[]{:T(128)}, f32[32,256]{1,0:T(8,128)S(1)}, s32[4,512,32]{1,2,0:T(8,128)S(1)}, ...), condition=%wide.region_8.9_spmd.clone, body=%wide.region_6.8_spmd.clone.sunk | while | flops 865075200 | bytes 1572959 | solution.py:63
  719.0 6.4 fusion.38
  725.4 7.5 fusion.39
  732.9 6.4 fusion.38
  739.3 7.5 fusion.39
  746.8 6.4 fusion.38
  753.2 7.5 fusion.39
  760.7 6.4 fusion.38
  767.1 7.5 fusion.39
  774.6 0.0 copy-start.3
  774.6 274.8 %psum.23 = f32[32,256]{1,0:T(8,128)S(1)} all-reduce(f32[32,256]{1,0:T(8,128)S(1)} %get-tuple-element.70), channel_id=1, replica_groups=mesh['rows'=64,'sub'=2] {'rows'}, use_global_device_ids=true, to_apply=%region_9.10 | all-reduce | flops 8192 | bytes 65536 | tf_op jit(solution)/shard_map/psum | solution.py:100
  1049.4 0.6 add_divide_fusion.2
  (30 shorter events, 0.2 us)
Async XLA Ops:
  8.6 21.0 %all-to-all-start = ((s32[128,8,1]{1,2,0:T(1,128)}), s32[128,8,1]{1,2,0:T(1,128)S(1)}, u32[]{:S(2)}, u32[]{:S(2)}) async-start(s32[128,8,1]{1,2,0:T(1,128)} %bitcast), calls=%async_computation | async-start | bytes 131072 | tf_op jit(solution)/shard_map/all_to_all | solution.py:76
  44.7 34.1 %all-to-all-start.1 = ((bf16[128,8,1024]{2,1,0:T(8,128)(2,1)}), bf16[128,8,1024]{2,1,0:T(8,128)(2,1)S(1)}, u32[]{:S(2)}, u32[]{:S(2)}) async-start(bf16[128,8,1024]{2,1,0:T(8,128)(2,1)} %bitcast.61), calls=%async_computation.1 | async-start | bytes 4194304 | tf_op jit(solution)/shard_map/all_to_all | solution.py:75
  78.9 1.4 copy-start.1
  80.2 33.3 %all-to-all-start.4 = ((s32[1024,2,32]{0,2,1:T(8,128)}), s32[1024,2,32]{0,2,1:T(8,128)S(1)}, u32[]{:S(2)}, u32[]{:S(2)}) async-start(s32[1024,2,32]{0,2,1:T(8,128)} %copy.34), calls=%async_computation.4 | async-start | bytes 524288 | tf_op jit(solution)/shard_map/all_to_all | solution.py:95
  86.8 5.5 copy-start
  113.5 28.5 %all-to-all-start.2 = ((bf16[1024,2,512]{2,0,1:T(8,128)(2,1)}), bf16[1024,2,512]{2,0,1:T(8,128)(2,1)S(1)}, u32[]{:S(2)}, u32[]{:S(2)}) async-start(bf16[1024,2,512]{2,0,1:T(8,128)(2,1)} %copy.31), calls=%async_computation.2 | async-start | bytes 4194304 | tf_op jit(solution)/shard_map/all_to_all | solution.py:94
  117.8 600.1 %all-reduce.2.cloned.1.call-start = ((), (), s32[]{:S(2)}) async-start(), calls=%async_computation.5 | async-start | bytes 1048576 | tf_op jit(solution)/shard_map/psum | solution.py:98
  153.2 564.6 %copy-start.2 = (f32[32,16,256]{2,1,0:T(8,128)S(1)}, f32[32,16,256]{2,1,0:T(8,128)}, u32[]{:S(2)}) copy-start(f32[32,16,256]{2,1,0:T(8,128)} %param.13) | copy-start | bytes 1572868
  175.3 0.8 copy-start.4
  774.6 275.4 %copy-start.3 = (f32[32,16,256]{2,1,0:T(8,128)}, f32[32,16,256]{2,1,0:T(8,128)S(1)}, u32[]{:S(2)}) copy-start(f32[32,16,256]{2,1,0:T(8,128)S(1)} %get-tuple-element.289) | copy-start | bytes 1572868
Sparse Core Ops, SparseCore 0:
  176.2 541.5 all-reduce.1
where the time goes:
time: 1060 us
  blocking collectives  562 us (53%)
  waiting for transfers between devices  324 us (31%)
  matrix products  73.2 us (7%)
  local copies, waits for them, and re-layouts  41.3 us (4%)
  starting transfers between devices  23.7 us (2%)
  other arithmetic  18.5 us (2%)
  between operations  14.2 us (1%)
    psum x1, blocking collectives, on_device(): lax.psum(error_pass(resid_half, code_half, code_levels, table), 'rows')  275 us
    psum x1, blocking collectives, on_device(): totals, tallies = lax.psum((totals, tallies), 'rows')  272 us
    psum x1, waiting for transfers between devices, on_device(): totals, tallies = lax.psum((totals, tallies), 'rows')  270 us
    dot_general x4, matrix products, error_add_block(): jnp.einsum('mkr,rm->mk', onehot, gap_norms, precision=lax.Precision.HIGHEST)  29.9 us
    dot_general x4, matrix products, error_add_block(): jnp.einsum('mkr,mdk->rmd', onehot, table, precision=lax.Precision.HIGHEST)  25.4 us
    all_to_all x1, waiting for transfers between devices, on_device(): lax.all_to_all(residual, 'sub', split_axis=1, concat_axis=0, tiled=True)  23.7 us
    all_to_all x1, waiting for transfers between devices, on_device(): lax.all_to_all(vectors, ('rows', 'sub'), split_axis=0, concat_axis=0, til...  22.3 us
  transfers between devices with their start and end apart: 5, of which 4 were waited for; matrix products, arithmetic and copies ran while one was open for 4% of the time, Pallas kernels for 0%

commit v1 on v0

v1 whole, which is shorter than its diff:
```python
import functools

import jax
import jax.numpy as jnp
from jax import lax
from jax.experimental import pallas as pl
from jax.experimental.pallas import tpu as pltpu
from jax.sharding import PartitionSpec as P

LANES = 128
COLS = 256


def split3(x):
    hi = x.astype(jnp.bfloat16)
    rest = x - hi.astype(jnp.float32)
    mid = rest.astype(jnp.bfloat16)
    lo = (rest - mid.astype(jnp.float32)).astype(jnp.bfloat16)
    return hi, mid, lo


def dot(a, b):
    return jnp.dot(a, b, preferred_element_type=jnp.float32)


def local_kernel(
    subs, width, prior_lists, v_ref, aux_ref, cent_ref, nc_ref, out_ref, hot, hot_t, cnt, code_t
):
    rows = v_ref.shape[0]
    lists = cent_ref.shape[0]
    levels = out_ref.shape[1] * LANES
    here = COLS // width
    step = pl.program_id(0)

    @pl.when(step == 0)
    def _():
        aux = aux_ref[...].astype(jnp.float32)
        aux_t = jnp.transpose(aux)
        row_ids = (aux_t[subs : subs + 1] * 256.0 + aux_t[subs + 1 : subs + 2]).astype(jnp.int32)
        col_ids = (aux[:, subs : subs + 1] * 256.0 + aux[:, subs + 1 : subs + 2]).astype(jnp.int32)
        level = lax.broadcasted_iota(jnp.int32, (lists, rows), 0)
        hot[...] = jnp.where(level == row_ids, 1.0, 0.0).astype(jnp.bfloat16)
        level = lax.broadcasted_iota(jnp.int32, (rows, lists), 1)
        hot_t[...] = jnp.where(level == col_ids, 1.0, 0.0).astype(jnp.bfloat16)
        cnt[...] = dot(hot[...], jnp.ones((rows, LANES), jnp.bfloat16))
        for block in range(subs // here):
            code_t[block] = aux_t[block * here : (block + 1) * here]

    v = v_ref[...]
    totals = dot(hot[...], v)
    counts = jnp.concatenate([cnt[...]] * (COLS // LANES), axis=1)
    nc = (totals + prior_lists * cent_ref[...].astype(jnp.float32)) / (counts + prior_lists)
    nc_ref[...] = nc
    hi, mid, lo = split3(nc)
    picked = (dot(hot_t[...], hi) + dot(hot_t[...], mid)) + dot(hot_t[...], lo)
    resid = (v.astype(jnp.float32) - picked).astype(jnp.bfloat16)

    wide = resid.astype(jnp.float32)
    square = wide * wide
    square_hi = square.astype(jnp.bfloat16)
    square_lo = (square - square_hi.astype(jnp.float32)).astype(jnp.bfloat16)
    source = lax.broadcasted_iota(jnp.int32, (COLS, LANES), 0) // width
    target = lax.broadcasted_iota(jnp.int32, (COLS, LANES), 1)
    spread = jnp.where((target % here == source) & (target < 3 * here), 1.0, 0.0).astype(
        jnp.bfloat16
    )
    norms = dot(square_hi, spread) + dot(square_lo, spread)
    n_hi, n_mid, n_lo = split3(norms)
    lane = lax.broadcasted_iota(jnp.int32, (rows, LANES), 1)
    extra = jnp.where(
        lane < here,
        n_hi.astype(jnp.float32),
        jnp.where(
            lane < 2 * here,
            n_mid.astype(jnp.float32),
            jnp.where(lane < 3 * here, n_lo.astype(jnp.float32), 1.0),
        ),
    ).astype(jnp.bfloat16)

    codes = code_t[step].astype(jnp.int32)
    level = lax.broadcasted_iota(jnp.int32, (levels, rows), 0)
    lane = lax.broadcasted_iota(jnp.int32, (levels, LANES), 1)
    group = LANES // width
    extra_sum = jnp.zeros((levels, LANES), jnp.float32)
    pieces = []
    for part in range(COLS // LANES):
        weights = jnp.concatenate(
            [resid[:, part * LANES : (part + 1) * LANES], extra], axis=1
        )
        sums = jnp.zeros((levels, LANES), jnp.float32)
        for k in range(group):
            i = part * group + k
            onehot = jnp.where(level == codes[i : i + 1], 1.0, 0.0).astype(jnp.bfloat16)
            found = dot(onehot, weights)
            sums = jnp.where(lane // width == k, found[:, :LANES], sums)
            extra_sum = jnp.where(lane % here == i, found[:, LANES:], extra_sum)
        pieces.append(jnp.transpose(sums))
    tail = jnp.transpose(extra_sum)
    norm_sum = (tail[:here] + tail[here : 2 * here]) + tail[2 * here : 3 * here]
    count_sum = tail[3 * here : 4 * here]
    blank = jnp.zeros((out_ref.shape[3] - width - 2, LANES), jnp.float32)
    for i in range(here):
        part, k = divmod(i, group)
        block = pieces[part][k * width : (k + 1) * width]
        for half in range(levels // LANES):
            at = slice(half * LANES, (half + 1) * LANES)
            out_ref[i, half, 0] = jnp.concatenate(
                [block[:, at], count_sum[i : i + 1, at], norm_sum[i : i + 1, at], blank], axis=0
            )


def local_pass(arrived, centroids, subs, width, levels, prior_lists, parts):
    rows = arrived.shape[0]
    lists, dims = centroids.shape
    here = COLS // width
    steps = dims // COLS
    per_part = steps // parts
    halves = levels // LANES
    held = 8 * (-(-(width + 2) // 8))
    return pl.pallas_call(
        functools.partial(local_kernel, subs, width, prior_lists),
        grid=(steps,),
        in_specs=[
            pl.BlockSpec((rows, COLS), lambda j: (0, j)),
            pl.BlockSpec((rows, LANES), lambda j: (0, dims // LANES)),
            pl.BlockSpec((lists, COLS), lambda j: (0, j)),
        ],
        out_specs=[
            pl.BlockSpec((lists, COLS), lambda j: (0, j)),
            pl.BlockSpec(
                (here, halves, 1, held, LANES),
                lambda j: (j % per_part, 0, j // per_part, 0, 0),
            ),
        ],
        out_shape=[
            jax.ShapeDtypeStruct((lists, dims), jnp.float32),
            jax.ShapeDtypeStruct((subs // parts, halves, parts, held, LANES), jnp.float32),
        ],
        scratch_shapes=[
            pltpu.VMEM((lists, rows), jnp.bfloat16),
            pltpu.VMEM((rows, lists), jnp.bfloat16),
            pltpu.VMEM((lists, LANES), jnp.float32),
            pltpu.VMEM((steps, here, rows), jnp.float32),
        ],
        compiler_params=pltpu.CompilerParams(vmem_limit_bytes=48 * 1024 * 1024),
        name="local_pass",
    )(arrived, arrived, centroids)


def owner_kernel(width, prior, part_ref, old_ref, out_ref):
    parts = part_ref[...]
    sums = parts[:, :width]
    counts = parts[:, width : width + 1]
    norms = parts[:, width + 1 : width + 2]
    total = jnp.sum(sums, axis=0)
    count = jnp.sum(counts, axis=0)
    new = (total + prior * old_ref[...]) / (count + prior)
    share = 1.0 / jnp.maximum(counts, 1.0)
    mean = sums * share
    gap = mean - new[None]
    inner = norms - jnp.sum(sums * mean, axis=1, keepdims=True)
    outer = counts * jnp.sum(gap * gap, axis=1, keepdims=True)
    errors = jnp.sum(jnp.maximum(inner, 0.0) + outer, axis=0)
    distortion = errors / (count + 1.0)
    blank = jnp.zeros((out_ref.shape[0] - width - 1, LANES), jnp.float32)
    out_ref[...] = jnp.concatenate([new, distortion, blank], axis=0)


def on_device(vectors, list_ids, codes, centroids, codebooks):
    rows, dims = vectors.shape
    owners = lax.axis_size("rows") * lax.axis_size("sub")
    lists = centroids.shape[0]
    subs = codes.shape[1]
    my_subs, width, levels = codebooks.shape
    halves = levels // LANES
    prior_lists = rows // lists
    prior_codes = rows * owners // levels
    local_ids = list_ids % lists
    aux = jnp.concatenate(
        [
            codes,
            (local_ids // 256)[:, None],
            (local_ids % 256)[:, None],
            jnp.zeros((rows, LANES - subs - 2), jnp.int32),
        ],
        axis=1,
    ).astype(jnp.bfloat16)
    sent = jnp.concatenate([vectors, aux], axis=1)
    arrived = lax.all_to_all(sent, ("rows", "sub"), split_axis=0, concat_axis=0, tiled=True)
    new_centroids, partials = local_pass(
        arrived, centroids, subs, width, levels, float(prior_lists), lax.axis_size("sub")
    )
    held = partials.shape[3]
    partials = partials.reshape(owners, held, LANES)
    mine = lax.all_to_all(partials, ("rows", "sub"), split_axis=0, concat_axis=0, tiled=True)
    place = lax.axis_index("rows")
    old = lax.dynamic_slice(
        codebooks, (place // halves, 0, (place % halves) * LANES), (1, width, LANES)
    )[0]
    done = pl.pallas_call(
        functools.partial(owner_kernel, width, float(prior_codes)),
        out_shape=jax.ShapeDtypeStruct((held, LANES), jnp.float32),
        compiler_params=pltpu.CompilerParams(vmem_limit_bytes=48 * 1024 * 1024),
        name="owner_pass",
    )(mine, old)
    copies = jnp.broadcast_to(done[None], (my_subs * halves, held, LANES))
    gathered = lax.all_to_all(copies, "rows", split_axis=0, concat_axis=0, tiled=True)
    gathered = gathered.reshape(my_subs, halves, held, LANES)
    table = jnp.transpose(gathered[:, :, :width], (0, 2, 1, 3)).reshape(my_subs, width, levels)
    distortion = gathered[:, :, width].reshape(my_subs, levels)
    return new_centroids, table, distortion


def solution(mesh):
    in_specs = (
        P(("rows", "sub"), None),
        P(("rows", "sub")),
        P(("rows", "sub"), None),
        P(("rows", "sub"), None),
        P("sub", None, None),
    )
    out_specs = (P(("rows", "sub"), None), P("sub", None, None), P("sub", None))
    return jax.shard_map(
        on_device, mesh=mesh, in_specs=in_specs, out_specs=out_specs, check_vma=False
    )
```

time: 1060 us -> 128 us (0.12)
  blocking collectives: 562 us -> 63.1 us
  waiting for transfers between devices: 324 us -> 24.1 us
  matrix products: 73.2 us -> 0 us
  local copies, waits for them, and re-layouts: 41.3 us -> 8.85 us
  Pallas kernels: 0 us -> 23.7 us
  starting transfers between devices: 23.7 us -> 5.24 us
  other arithmetic: 18.5 us -> 1.73 us
  between operations: 14.2 us -> 0.75 us
    psum x2 -> x0, blocking collectives: 547 us -> none  [the longest x1 275 us: on_device(): lax.psum(error_pass(resid_half, code_half, code_levels, table), 'rows')]
    psum x1 -> x0, waiting for transfers between devices: 270 us -> none  [on_device(): totals, tallies = lax.psum((totals, tallies), 'rows')]
    dot_general x13 -> x0, matrix products: 73.2 us -> none  [the longest x4 29.9 us: error_add_block(): jnp.einsum('mkr,rm->mk', onehot, gap_norms, precision=lax.Precision.HIGHEST)]
    all_to_all x1 -> x2, blocking collectives: 15.1 us -> 63.1 us  [the longest x1 43.6 us: on_device(): lax.all_to_all(sent, ('rows', 'sub'), split_axis=0, concat_axis=0, tiled=...]
    all_to_all x4 -> x1, waiting for transfers between devices: 54 us -> 24.1 us  [on_device(): lax.all_to_all(partials, ('rows', 'sub'), split_axis=0, concat_axis=0, ti...]
    pallas_call x0 -> x2, Pallas kernels: none -> 23.7 us  [the longest x1 22.8 us: local_pass(): pl.pallas_call(functools.partial(local_kernel, subs, width, prior_lists),...]
    all_to_all x4 -> x1, starting transfers between devices: 23.6 us -> 5.24 us  [on_device(): lax.all_to_all(partials, ('rows', 'sub'), split_axis=0, concat_axis=0, ti...]
    gather x2 -> x0, local copies, waits for them, and re-layouts: 12 us -> none  [on_device(): jnp.take(new_centroids, arrived_ids, axis=0)]
  transfers between devices with their start and end apart: 5 -> 1, of which waited for: 4 -> 1; matrix products, arithmetic and copies ran while one was open for 4% -> 0% of each run, Pallas kernels for 0% -> 0%
where the time goes in v1:
time: 128 us
  blocking collectives  63.1 us (49%)
  waiting for transfers between devices  24.1 us (19%)
  Pallas kernels  23.7 us (19%)
  local copies, waits for them, and re-layouts  8.85 us (7%)
  starting transfers between devices  5.24 us (4%)
  other arithmetic  1.73 us (1%)
    all_to_all x1, blocking collectives, on_device(): lax.all_to_all(sent, ('rows', 'sub'), split_axis=0, concat_axis=0, tiled=...  43.6 us
    all_to_all x1, waiting for transfers between devices, on_device(): lax.all_to_all(partials, ('rows', 'sub'), split_axis=0, concat_axis=0, ti...  24.1 us
    pallas_call x1, Pallas kernels, local_pass(): pl.pallas_call(functools.partial(local_kernel, subs, width, prior_lists),...  22.8 us
    all_to_all x1, blocking collectives, on_device(): lax.all_to_all(copies, 'rows', split_axis=0, concat_axis=0, tiled=True)  19.4 us
    all_to_all x1, starting transfers between devices, on_device(): lax.all_to_all(partials, ('rows', 'sub'), split_axis=0, concat_axis=0, ti...  5.24 us
    concatenate x1, local copies, waits for them, and re-layouts, on_device(): sent = jnp.concatenate([vectors, aux], axis=1)  4.03 us
  transfers between devices with their start and end apart: 1, of which 1 were waited for; matrix products, arithmetic and copies ran while one was open for 0% of the time, Pallas kernels for 0%

profile of v1, /device:TPU:1, one launch (start us, length us, event | category | flops | bytes accessed | tf_op | source)
XLA Modules:
  0.0 127.5 jit_solution(11077596417441315775)
XLA Ops:
  0.6 0.0 copy-start
  0.6 1.0 convert.13
  1.7 0.2 copy.14
  1.8 0.7 fusion.2
  2.6 0.2 broadcast_in_dim.21
  2.8 0.9 broadcast_in_dim.22
  3.7 0.7 broadcast_in_dim.19
  4.4 4.0 %concatenate.6 = bf16[1024,1152]{1,0:T(8,128)(2,1)S(1)} concatenate(bf16[1024,1024]{1,0:T(8,128)(2,1)} %param.5, bf16[1024,64]{1,0:T(8,128)(2,1)S(1)} %copy.14, bf16[1024,1]{1,0:T(8,128)(2,1)S(1)} %broadcast_in_dim.21, bf16[1024,1]{1,0:T(8,128)(2,1)} %broadcast_in_dim.22, bf16[1024,62]{1,0:T(8,128)(2,1)} %broadcast_in_dim.19), dimensions={1} | concatenate | bytes 4718592 | tf_op jit(solution)/shard_map/concatenate | solution.py:188
  8.4 0.0 copy-start.2
  8.5 43.6 %all_to_all.21 = bf16[128,8,1152]{2,1,0:T(8,128)(2,1)S(1)} all-to-all(bf16[128,8,1152]{2,1,0:T(8,128)(2,1)S(1)} %bitcast.19), channel_id=1, replica_groups=mesh['rows'=64,'sub'=2] {'rows','sub'}, dimensions={0} | all-to-all | bytes 4718592 | tf_op jit(solution)/shard_map/all_to_all | solution.py:189
  52.1 0.0 copy-done.2
  52.1 22.8 %local_pass.1 = (f32[512,1024]{1,0:T(8,128)}, f32[32,2,2,24,128]{4,3,2,1,0:T(8,128)S(1)}) custom-call(bf16[1024,1152]{1,0:T(8,128)(2,1)S(1)} %bitcast.16, bf16[1024,1152]{1,0:T(8,128)(2,1)S(1)} %bitcast.17, bf16[512,1024]{1,0:T(8,128)(2,1)S(1)} %copy-done.2), custom_call_target="tpu_custom_call" | custom-call | tf_op jit(solution)/shard_map/local_pass/pallas_call | solution.py:120
  74.9 0.0 copy-start.1
  74.9 1.2 copy-done.1
  76.0 5.2 %all-to-all-start.1 = ((f32[128,24,128]{2,1,0:T(8,128)}), f32[128,24,128]{2,1,0:T(8,128)S(1)}, u32[]{:S(2)}, u32[]{:S(2)}) async-start(f32[128,24,128]{2,1,0:T(8,128)} %bitcast.18), calls=%async_computation.1 | async-start | bytes 3145728 | tf_op jit(solution)/shard_map/all_to_all | solution.py:195
  81.3 0.0 copy-done
  81.3 24.1 %all-to-all-done.1.part_ref = f32[128,24,128]{2,1,0:T(8,128)S(1)} async-done(((f32[128,24,128]{2,1,0:T(8,128)}), f32[128,24,128]{2,1,0:T(8,128)S(1)}, u32[]{:S(2)}, u32[]{:S(2)}) %all-to-all-start.1) | async-done | bytes 1572896 | tf_op jit(solution)/shard_map/all_to_all | solution.py:195
  105.5 1.0 owner_pass.1
  106.5 0.1 broadcast_in_dim.20
  106.5 19.4 %all_to_all.22 = f32[64,24,128]{2,1,0:T(8,128)S(1)} all-to-all(f32[64,24,128]{2,1,0:T(8,128)S(1)} %broadcast_in_dim.20), channel_id=1, replica_groups=mesh['rows'=64,'sub'=2] {'rows'}, dimensions={0} | all-to-all | bytes 1572864 | tf_op jit(solution)/shard_map/all_to_all | solution.py:207
  126.0 0.9 copy_bitcast_fusion
  126.8 0.1 slice_reduce_fusion
  126.9 0.6 copy.22
  (1 shorter events, 0.0 us)
Async XLA Ops:
  0.6 80.7 %copy-start = (f32[32,16,256]{2,1,0:T(8,128)S(1)}, f32[32,16,256]{2,1,0:T(8,128)}, u32[]{:S(2)}) copy-start(f32[32,16,256]{2,1,0:T(8,128)} %param.9) | copy-start | bytes 1572868
  8.4 43.7 %copy-start.2 = (bf16[512,1024]{1,0:T(8,128)(2,1)S(1)}, bf16[512,1024]{1,0:T(8,128)(2,1)}, u32[]{:S(2)}) copy-start(bf16[512,1024]{1,0:T(8,128)(2,1)} %cent_ref.1) | copy-start | bytes 3145732
  74.9 1.2 copy-start.1
  76.0 29.4 %all-to-all-start.1 = ((f32[128,24,128]{2,1,0:T(8,128)}), f32[128,24,128]{2,1,0:T(8,128)S(1)}, u32[]{:S(2)}, u32[]{:S(2)}) async-start(f32[128,24,128]{2,1,0:T(8,128)} %bitcast.18), calls=%async_computation.1 | async-start | bytes 3145728 | tf_op jit(solution)/shard_map/all_to_all | solution.py:195

commit v2 on v0

v2 whole, which is shorter than its diff:
```python
import functools

import jax
import jax.numpy as jnp
from jax import lax
from jax.experimental import pallas as pl
from jax.experimental.pallas import tpu as pltpu
from jax.sharding import Mesh, PartitionSpec as P

LANES = 128
COLS = 256
CORES = 2
MIB = 1024 * 1024
IN_VMEM = pl.BlockSpec(memory_space=pltpu.VMEM)
SPLIT = ("chip", "core", "sub")


def split3(x):
    hi = x.astype(jnp.bfloat16)
    rest = x - hi.astype(jnp.float32)
    mid = rest.astype(jnp.bfloat16)
    lo = (rest - mid.astype(jnp.float32)).astype(jnp.bfloat16)
    return hi, mid, lo


def dot(a, b):
    return jnp.dot(a, b, preferred_element_type=jnp.float32)


def pack_kernel(lists, v_ref, ids_ref, codes_ref, out_ref, sem):
    rows, dims = v_ref.shape
    subs = codes_ref.shape[0]
    copy = pltpu.make_async_copy(v_ref, out_ref.at[:, :dims], sem)
    copy.start()
    ids = lax.rem(ids_ref[...], lists)
    high = lax.div(ids, 256)
    aux = jnp.concatenate(
        [
            codes_ref[...].astype(jnp.float32),
            high.astype(jnp.float32),
            (ids - 256 * high).astype(jnp.float32),
            jnp.zeros((LANES - subs - 2, rows), jnp.float32),
        ],
        axis=0,
    )
    out_ref[:, dims:] = jnp.transpose(aux).astype(jnp.bfloat16)
    copy.wait()


def pack(vectors, list_ids, codes, lists):
    rows, dims = vectors.shape
    return pl.pallas_call(
        functools.partial(pack_kernel, lists),
        in_specs=[pl.BlockSpec(memory_space=pl.ANY), IN_VMEM, IN_VMEM],
        out_specs=IN_VMEM,
        out_shape=jax.ShapeDtypeStruct((rows, dims + LANES), jnp.bfloat16),
        scratch_shapes=[pltpu.SemaphoreType.DMA],
        compiler_params=pltpu.CompilerParams(vmem_limit_bytes=12 * MIB),
        name="pack",
    )(vectors, list_ids.reshape(1, rows), jnp.transpose(codes))


def local_kernel(
    subs,
    width,
    parts,
    prior,
    chunk,
    core_ref,
    arr_ref,
    cent_ref,
    nc_ref,
    keep_ref,
    give_ref,
    hot,
    inv,
    code_t,
    table,
    picked,
    resid,
    extra,
    ids_v,
    ids_s,
    sem,
):
    rows = arr_ref.shape[0]
    lists, dims = cent_ref.shape
    levels = 2 * LANES
    here = COLS // width
    group = LANES // width
    tiles = dims // LANES
    side = COLS // LANES
    held = width + 2
    first_core = core_ref[0] == 0

    aux = arr_ref[:, dims:].astype(jnp.float32)
    aux_t = jnp.transpose(aux)
    row_ids = (aux_t[subs : subs + 1] * 256.0 + aux_t[subs + 1 : subs + 2]).astype(jnp.int32)
    ids_v[...] = row_ids * tiles
    copy = pltpu.make_async_copy(ids_v, ids_s, sem)
    copy.start()
    level = lax.broadcasted_iota(jnp.int32, (lists, rows), 0)
    hot[...] = jnp.where(level == row_ids, 1.0, 0.0).astype(jnp.bfloat16)
    counts = dot(hot[...], jnp.ones((rows, LANES), jnp.bfloat16))
    inv[...] = 1.0 / (counts + prior)
    for b in range(subs // here):
        code_t[b] = aux_t[b * here : (b + 1) * here].astype(jnp.int32)

    for j in range(dims // COLS):
        totals = dot(hot[...], arr_ref[:, j * COLS : (j + 1) * COLS])
        for h in range(side):
            tile = j * side + h
            at = slice(tile * LANES, (tile + 1) * LANES)
            old = cent_ref[:, at].astype(jnp.float32)
            nc = (totals[:, h * LANES : (h + 1) * LANES] + prior * old) * inv[...]
            nc_ref[:, at] = nc
            table[pl.ds(tile, lists, stride=tiles), :] = nc
    copy.wait()

    def pick(q, _):
        for u in range(8):
            r = q * 8 + u
            row = table[pl.ds(pl.multiple_of(ids_s[0, r], 8), tiles), :]
            picked[pl.ds(pl.multiple_of(r * tiles, 8), tiles), :] = row
        return 0

    lax.fori_loop(0, rows // 8, pick, 0)

    source = lax.broadcasted_iota(jnp.int32, (COLS, LANES), 0) // width
    target = lax.broadcasted_iota(jnp.int32, (COLS, LANES), 1)
    spread = jnp.where((target % here == source) & (target < 3 * here), 1.0, 0.0).astype(
        jnp.bfloat16
    )

    def columns(j, _):
        at = pl.ds(pl.multiple_of(j * COLS, COLS), COLS)
        for i in range(rows // chunk):
            ra = slice(i * chunk, (i + 1) * chunk)
            near = jnp.concatenate(
                [
                    picked[pl.ds(i * chunk * tiles + j * side + h, chunk, stride=tiles), :]
                    for h in range(side)
                ],
                axis=1,
            )
            r = (arr_ref[ra, at].astype(jnp.float32) - near).astype(jnp.bfloat16)
            resid[ra, :] = r
            wide = r.astype(jnp.float32)
            square = wide * wide
            square_hi = square.astype(jnp.bfloat16)
            square_lo = (square - square_hi.astype(jnp.float32)).astype(jnp.bfloat16)
            n_hi, n_mid, n_lo = split3(dot(square_hi, spread) + dot(square_lo, spread))
            lane = lax.broadcasted_iota(jnp.int32, (chunk, LANES), 1)
            extra[ra, :] = jnp.where(
                lane < here,
                n_hi.astype(jnp.float32),
                jnp.where(
                    lane < 2 * here,
                    n_mid.astype(jnp.float32),
                    jnp.where(lane < 3 * here, n_lo.astype(jnp.float32), 1.0),
                ),
            ).astype(jnp.bfloat16)

        codes = code_t[j]
        level = lax.broadcasted_iota(jnp.int32, (levels, rows), 0)
        lane = lax.broadcasted_iota(jnp.int32, (levels, LANES), 1)
        extra_sum = jnp.zeros((levels, LANES), jnp.float32)
        pieces = []
        for part in range(side):
            weights = jnp.concatenate(
                [resid[:, part * LANES : (part + 1) * LANES], extra[...]], axis=1
            )
            sums = jnp.zeros((levels, LANES), jnp.float32)
            for k in range(group):
                i = part * group + k
                onehot = jnp.where(level == codes[i : i + 1], 1.0, 0.0).astype(jnp.bfloat16)
                found = dot(onehot, weights)
                sums = jnp.where(lane // width == k, found[:, :LANES], sums)
                extra_sum = jnp.where(lane % here == i, found[:, LANES:], extra_sum)
            pieces.append(jnp.transpose(sums))
        tail = jnp.transpose(extra_sum)
        norm_sum = (tail[:here] + tail[here : 2 * here]) + tail[2 * here : 3 * here]
        count_sum = tail[3 * here : 4 * here]
        steps = subs // parts // here
        for i in range(here):
            part, k = divmod(i, group)
            block = jnp.concatenate(
                [
                    pieces[part][k * width : (k + 1) * width],
                    count_sum[i : i + 1],
                    norm_sum[i : i + 1],
                ],
                axis=0,
            )
            left, right = block[:, :LANES], block[:, LANES:]
            at_row = ((lax.rem(j, steps) * here + i) * parts + lax.div(j, steps)) * held
            keep_ref[pl.ds(at_row, held), :] = jnp.where(first_core, left, right)
            give_ref[pl.ds(at_row, held), :] = jnp.where(first_core, right, left)
        return 0

    lax.fori_loop(0, dims // COLS, columns, 0)


def local_pass(core, arrived, centroids, subs, width, prior, parts):
    rows = arrived.shape[0]
    lists, dims = centroids.shape
    tiles = dims // LANES
    here = COLS // width
    sums = jax.ShapeDtypeStruct((subs * (width + 2), LANES), jnp.float32)
    return pl.pallas_call(
        functools.partial(local_kernel, subs, width, parts, prior, 256),
        in_specs=[pl.BlockSpec(memory_space=pltpu.SMEM), IN_VMEM, IN_VMEM],
        out_specs=[IN_VMEM, IN_VMEM, IN_VMEM],
        out_shape=[jax.ShapeDtypeStruct((lists, dims), jnp.float32), sums, sums],
        scratch_shapes=[
            pltpu.VMEM((lists, rows), jnp.bfloat16),
            pltpu.VMEM((lists, LANES), jnp.float32),
            pltpu.VMEM((subs // here, here, rows), jnp.int32),
            pltpu.VMEM((lists * tiles, LANES), jnp.float32),
            pltpu.VMEM((rows * tiles, LANES), jnp.float32),
            pltpu.VMEM((rows, COLS), jnp.bfloat16),
            pltpu.VMEM((rows, LANES), jnp.bfloat16),
            pltpu.VMEM((1, rows), jnp.int32),
            pltpu.SMEM((1, rows), jnp.int32),
            pltpu.SemaphoreType.DMA,
        ],
        compiler_params=pltpu.CompilerParams(vmem_limit_bytes=32 * MIB),
        name="local_pass",
    )(core, arrived, centroids)


def owner_kernel(width, prior, copies, part_ref, old_ref, out_ref):
    held = width + 2
    sources = part_ref.shape[0] // held
    taken = [part_ref[pl.ds(i, sources, stride=held), :] for i in range(held)]
    sums, counts, norms = taken[:width], taken[width], taken[width + 1]
    count = jnp.sum(counts, axis=0, keepdims=True)
    share = 1.0 / jnp.maximum(counts, 1.0)
    inner = norms
    outer = jnp.zeros_like(norms)
    rows = []
    for d in range(width):
        total = jnp.sum(sums[d], axis=0, keepdims=True)
        new = (total + prior * old_ref[d : d + 1]) / (count + prior)
        mean = sums[d] * share
        gap = mean - new
        inner = inner - sums[d] * mean
        outer = outer + gap * gap
        rows.append(new)
    errors = jnp.sum(jnp.maximum(inner, 0.0) + counts * outer, axis=0, keepdims=True)
    rows.append(errors / (count + 1.0))
    result = jnp.concatenate(rows, axis=0)
    for c in range(copies):
        out_ref[c * (width + 1) : (c + 1) * (width + 1)] = result


def finish_kernel(width, core_ref, mine_ref, other_ref, table_ref, dist_ref):
    held = width + 1
    subs = table_ref.shape[0]
    first_core = core_ref[0] == 0
    for ref, at in ((0, slice(0, LANES)), (1, slice(LANES, 2 * LANES))):
        own = first_core if ref == 0 else jnp.logical_not(first_core)
        for m in range(subs):
            rows = slice(m * held, m * held + width)
            table_ref[m, :, at] = jnp.where(own, mine_ref[rows], other_ref[rows])
        last = pl.ds(width, subs, stride=held)
        dist_ref[:, at] = jnp.where(own, mine_ref[last, :], other_ref[last, :])


def on_device(vectors, list_ids, codes, centroids, codebooks):
    rows, dims = vectors.shape
    chips = lax.axis_size("chip")
    parts = lax.axis_size("sub")
    owners = chips * CORES * parts
    lists = centroids.shape[0]
    subs = codes.shape[1]
    my_subs, width, levels = codebooks.shape
    prior_lists = float(rows // lists)
    prior_codes = float(rows * owners // levels)
    core = lax.axis_index("core")
    core_arg = core.astype(jnp.int32).reshape(1)
    swap = [(0, 1), (1, 0)]

    sent = pack(vectors, list_ids, codes, lists)
    arrived = lax.all_to_all(sent, SPLIT, split_axis=0, concat_axis=0, tiled=True)
    new_centroids, keep, give = local_pass(
        core_arg, arrived, centroids, subs, width, prior_lists, parts
    )
    paired = keep + lax.ppermute(give, "core", swap)
    held = width + 2
    mine = lax.all_to_all(
        paired.reshape(chips * parts, 1, held * LANES),
        ("chip", "sub"),
        split_axis=0,
        concat_axis=0,
        tiled=True,
    ).reshape(chips * parts * held, LANES)
    old = lax.dynamic_slice(
        codebooks, (lax.axis_index("chip"), 0, core * LANES), (1, width, LANES)
    )[0]
    held = width + 1
    done = pl.pallas_call(
        functools.partial(owner_kernel, width, prior_codes, chips),
        in_specs=[IN_VMEM, IN_VMEM],
        out_specs=IN_VMEM,
        out_shape=jax.ShapeDtypeStruct((chips * held, LANES), jnp.float32),
        compiler_params=pltpu.CompilerParams(vmem_limit_bytes=8 * MIB),
        name="owner_pass",
    )(mine, old)
    half = lax.all_to_all(
        done.reshape(chips, 1, held * LANES), "chip", split_axis=0, concat_axis=0, tiled=True
    ).reshape(chips * held, LANES)
    other = lax.ppermute(half, "core", swap)
    table, distortion = pl.pallas_call(
        functools.partial(finish_kernel, width),
        in_specs=[pl.BlockSpec(memory_space=pltpu.SMEM), IN_VMEM, IN_VMEM],
        out_specs=[IN_VMEM, IN_VMEM],
        out_shape=[
            jax.ShapeDtypeStruct((my_subs, width, levels), jnp.float32),
            jax.ShapeDtypeStruct((my_subs, levels), jnp.float32),
        ],
        compiler_params=pltpu.CompilerParams(vmem_limit_bytes=8 * MIB),
        name="finish",
    )(core_arg, half, other)
    return new_centroids, table, distortion


def solution(mesh):
    parts = mesh.shape["sub"]
    cores = Mesh(mesh.devices.reshape(-1, CORES, parts), SPLIT)
    in_specs = (
        P(SPLIT, None),
        P(SPLIT),
        P(SPLIT, None),
        P(SPLIT, None),
        P("sub", None, None),
    )
    out_specs = (P(SPLIT, None), P("sub", None, None), P("sub", None))
    return jax.shard_map(
        on_device, mesh=cores, in_specs=in_specs, out_specs=out_specs, check_vma=False
    )
```

time: 1060 us -> 105 us (0.10)
  blocking collectives: 562 us -> 11.2 us
  waiting for transfers between devices: 324 us -> 48.1 us
  matrix products: 73.2 us -> 0 us
  local copies, waits for them, and re-layouts: 41.3 us -> 5.93 us
  other arithmetic: 18.5 us -> 0.87 us
  Pallas kernels: 0 us -> 16.2 us
  between operations: 14.2 us -> 0.73 us
    psum x2 -> x0, blocking collectives: 547 us -> none  [the longest x1 275 us: on_device(): lax.psum(error_pass(resid_half, code_half, code_levels, table), 'rows')]
    psum x1 -> x0, waiting for transfers between devices: 270 us -> none  [on_device(): totals, tallies = lax.psum((totals, tallies), 'rows')]
    dot_general x13 -> x0, matrix products: 73.2 us -> none  [the longest x4 29.9 us: error_add_block(): jnp.einsum('mkr,rm->mk', onehot, gap_norms, precision=lax.Precision.HIGHEST)]
    pallas_call x0 -> x4, Pallas kernels: none -> 16.2 us  [the longest x1 14.8 us: local_pass(): pl.pallas_call(functools.partial(local_kernel, subs, width, parts, prior,...]
    gather x2 -> x0, local copies, waits for them, and re-layouts: 12 us -> none  [on_device(): jnp.take(new_centroids, arrived_ids, axis=0)]
    all_to_all x4 -> x2, waiting for transfers between devices: 54 us -> 45.2 us  [the longest x1 32.3 us: on_device(): lax.all_to_all(sent, SPLIT, split_axis=0, concat_axis=0, tiled=True)]
    all_to_all x4 -> x2, starting transfers between devices: 23.6 us -> 16.4 us  [the longest x1 11.5 us: on_device(): lax.all_to_all(sent, SPLIT, split_axis=0, concat_axis=0, tiled=True)]
  transfers between devices with their start and end apart: 5 -> 4, of which waited for: 4 -> 4; matrix products, arithmetic and copies ran while one was open for 4% -> 0% of each run, Pallas kernels for 0% -> 0%
where the time goes in v2:
time: 105 us; the launch traced here: 104 us
  waiting for transfers between devices  48.1 us (46%)
  starting transfers between devices  21.4 us (20%)
  Pallas kernels  16.2 us (15%)
  blocking collectives  11.2 us (11%)
  local copies, waits for them, and re-layouts  5.93 us (6%)
    all_to_all x1, waiting for transfers between devices, on_device(): lax.all_to_all(sent, SPLIT, split_axis=0, concat_axis=0, tiled=True)  32.3 us
    pallas_call x1, Pallas kernels, local_pass(): pl.pallas_call(functools.partial(local_kernel, subs, width, parts, prior,...  14.8 us
    all_to_all x1, waiting for transfers between devices, on_device(): lax.all_to_all(paired.reshape(chips * parts, 1, held * LANES), ('chip', '...  12.9 us
    all_to_all x1, starting transfers between devices, on_device(): lax.all_to_all(sent, SPLIT, split_axis=0, concat_axis=0, tiled=True)  11.5 us
    all_to_all x1, blocking collectives, on_device(): lax.all_to_all(done.reshape(chips, 1, held * LANES), 'chip', split_axis=0...  11.2 us
    unnamed x12, local copies, waits for them, and re-layouts  5.92 us
    all_to_all x1, starting transfers between devices, on_device(): lax.all_to_all(paired.reshape(chips * parts, 1, held * LANES), ('chip', '...  4.87 us
    ppermute x1, starting transfers between devices, on_device(): other = lax.ppermute(half, 'core', swap)  3.43 us
  transfers between devices with their start and end apart: 4, of which 4 were waited for; matrix products, arithmetic and copies ran while one was open for 0% of the time, Pallas kernels for 0%

profile of v2, /device:TPU:1, one launch (start us, length us, event | category | flops | bytes accessed | tf_op | source)
XLA Modules:
  0.0 104.4 jit_solution(5490046822379930778)
XLA Ops:
  0.6 0.0 copy-start
  0.6 0.0 copy-start.2
  0.7 1.6 %copy-done.2 = bf16[1024,1024]{1,0:T(8,128)(2,1)S(1)} copy-done((bf16[1024,1024]{1,0:T(8,128)(2,1)S(1)}, bf16[1024,1024]{1,0:T(8,128)(2,1)}, u32[]{:S(2)}) %copy-start.2) | copy-done | bytes 2097176
  2.3 0.0 copy-start.4
  2.3 0.9 copy-done.4
  3.2 0.0 copy-start.5
  3.2 0.7 copy-done.5
  3.9 0.4 pack.1
  4.4 0.0 copy-start.1
  4.4 1.4 %copy-done.1 = bf16[1024,1152]{1,0:T(8,128)(2,1)} copy-done((bf16[1024,1152]{1,0:T(8,128)(2,1)}, bf16[1024,1152]{1,0:T(8,128)(2,1)S(1)}, u32[]{:S(2)}) %copy-start.1) | copy-done | bytes 2359320
  5.8 11.5 %all-to-all-start = ((bf16[128,8,1152]{2,1,0:T(8,128)(2,1)}), bf16[128,8,1152]{2,1,0:T(8,128)(2,1)S(1)}, u32[]{:S(2)}, u32[]{:S(2)}) async-start(bf16[128,8,1152]{2,1,0:T(8,128)(2,1)} %bitcast.12), calls=%async_computation | async-start | bytes 4718592 | tf_op jit(solution)/shard_map/all_to_all | solution.py:285
  17.3 32.3 %all-to-all-done = bf16[128,8,1152]{2,1,0:T(8,128)(2,1)S(1)} async-done(((bf16[128,8,1152]{2,1,0:T(8,128)(2,1)}), bf16[128,8,1152]{2,1,0:T(8,128)(2,1)S(1)}, u32[]{:S(2)}, u32[]{:S(2)}) %all-to-all-start) | async-done | bytes 2359328 | tf_op jit(solution)/shard_map/all_to_all | solution.py:285
  49.6 0.0 copy-start.3
  49.6 1.2 %copy-done.3 = bf16[512,1024]{1,0:T(8,128)(2,1)S(1)} copy-done((bf16[512,1024]{1,0:T(8,128)(2,1)S(1)}, bf16[512,1024]{1,0:T(8,128)(2,1)}, u32[]{:S(2)}) %copy-start.3) | copy-done | bytes 1048600
  50.8 14.8 %local_pass.1 = (f32[512,1024]{1,0:T(8,128)}, f32[1152,128]{1,0:T(8,128)S(1)}, f32[1152,128]{1,0:T(8,128)S(1)}) custom-call(s32[1]{0:T(128)} %bitcast.core_ref, bf16[1024,1152]{1,0:T(8,128)(2,1)S(1)} %bitcast.11, bf16[512,1024]{1,0:T(8,128)(2,1)S(1)} %copy-done.3), custom_call_target="tpu_custom_call" | custom-call | tf_op jit(solution)/shard_map/local_pass/pallas_call | solution.py:210
  65.6 1.6 %collective-permute-start = (f32[1152,128]{1,0:T(8,128)S(1)}, f32[1152,128]{1,0:T(8,128)S(1)}, u32[]{:S(2)}, u32[]{:S(2)}) collective-permute-start(f32[1152,128]{1,0:T(8,128)S(1)} %get-tuple-element.10), channel_id=1, source_target_pairs={{0,2},{2,0},{1,3},{3,1},{4,6},{6,4},{5,7},{7,5},{8,10},{10,8},{9,1... | collective-permute-start | bytes 1769480 | tf_op jit(solution)/shard_map/ppermute | solution.py:289
  67.3 1.6 %collective-permute-done = f32[1152,128]{1,0:T(8,128)S(1)} collective-permute-done((f32[1152,128]{1,0:T(8,128)S(1)}, f32[1152,128]{1,0:T(8,128)S(1)}, u32[]{:S(2)}, u32[]{:S(2)}) %collective-permute-start) | collective-permute-done | bytes 589856 | tf_op jit(solution)/shard_map/ppermute | solution.py:289
  68.9 0.9 add.9
  69.8 4.9 %all-to-all-start.1 = ((f32[64,1,2304]{2,1,0:T(1,128)}), f32[64,1,2304]{2,1,0:T(1,128)S(1)}, u32[]{:S(2)}, u32[]{:S(2)}) async-start(f32[64,1,2304]{2,1,0:T(1,128)} %bitcast.5), calls=%async_computation.1 | async-start | bytes 1179648 | tf_op jit(solution)/shard_map/all_to_all | solution.py:291
  74.6 0.0 copy-done
  74.7 12.9 %all-to-all-done.1 = f32[64,1,2304]{2,1,0:T(1,128)S(1)} async-done(((f32[64,1,2304]{2,1,0:T(1,128)}), f32[64,1,2304]{2,1,0:T(1,128)S(1)}, u32[]{:S(2)}, u32[]{:S(2)}) %all-to-all-start.1) | async-done | bytes 589856 | tf_op jit(solution)/shard_map/all_to_all | solution.py:291
  87.6 0.2 owner_pass.1
  87.8 11.2 %all_to_all.21 = f32[32,1,2176]{2,1,0:T(1,128)S(1)} all-to-all(f32[32,1,2176]{2,1,0:T(1,128)S(1)} %bitcast.16), channel_id=1, replica_groups=mesh['chip'=32,'core'=2,'sub'=2] {'chip'}, dimensions={0} | all-to-all | bytes 557056 | tf_op jit(solution)/shard_map/all_to_all | solution.py:310
  98.9 3.4 %collective-permute-start.1 = (f32[544,128]{1,0:T(8,128)S(1)}, f32[544,128]{1,0:T(8,128)S(1)}, u32[]{:S(2)}, u32[]{:S(2)}) collective-permute-start(f32[544,128]{1,0:T(8,128)S(1)} %bitcast.14), channel_id=1, source_target_pairs={{0,2},{2,0},{1,3},{3,1},{4,6},{6,4},{5,7},{7,5},{8,10},{10,8},{9,1... | collective-permute-start | bytes 835592 | tf_op jit(solution)/shard_map/ppermute | solution.py:313
  102.4 1.2 %collective-permute-done.1.other_ref = f32[544,128]{1,0:T(8,128)S(1)} collective-permute-done((f32[544,128]{1,0:T(8,128)S(1)}, f32[544,128]{1,0:T(8,128)S(1)}, u32[]{:S(2)}, u32[]{:S(2)}) %collective-permute-start.1) | collective-permute-done | bytes 278560 | tf_op jit(solution)/shard_map/ppermute | solution.py:313
  103.6 0.8 finish.1
  (1 shorter events, 0.0 us)
Async XLA Ops:
  0.6 74.0 %copy-start = (f32[32,16,256]{2,1,0:T(8,128)S(1)}, f32[32,16,256]{2,1,0:T(8,128)}, u32[]{:S(2)}) copy-start(f32[32,16,256]{2,1,0:T(8,128)} %param.9) | copy-start | bytes 1572868
  0.6 1.6 %copy-start.2 = (bf16[1024,1024]{1,0:T(8,128)(2,1)S(1)}, bf16[1024,1024]{1,0:T(8,128)(2,1)}, u32[]{:S(2)}) copy-start(bf16[1024,1024]{1,0:T(8,128)(2,1)} %v_ref.1) | copy-start | bytes 6291460
  2.3 0.9 copy-start.4
  3.2 0.7 copy-start.5
  4.4 1.4 %copy-start.1 = (bf16[1024,1152]{1,0:T(8,128)(2,1)}, bf16[1024,1152]{1,0:T(8,128)(2,1)S(1)}, u32[]{:S(2)}) copy-start(bf16[1024,1152]{1,0:T(8,128)(2,1)S(1)} %pack.1) | copy-start | bytes 7077892
  5.8 43.8 %all-to-all-start = ((bf16[128,8,1152]{2,1,0:T(8,128)(2,1)}), bf16[128,8,1152]{2,1,0:T(8,128)(2,1)S(1)}, u32[]{:S(2)}, u32[]{:S(2)}) async-start(bf16[128,8,1152]{2,1,0:T(8,128)(2,1)} %bitcast.12), calls=%async_computation | async-start | bytes 4718592 | tf_op jit(solution)/shard_map/all_to_all | solution.py:285
  49.6 1.2 %copy-start.3 = (bf16[512,1024]{1,0:T(8,128)(2,1)S(1)}, bf16[512,1024]{1,0:T(8,128)(2,1)}, u32[]{:S(2)}) copy-start(bf16[512,1024]{1,0:T(8,128)(2,1)} %cent_ref.1) | copy-start | bytes 3145732
  65.6 3.3 %collective-permute-start = (f32[1152,128]{1,0:T(8,128)S(1)}, f32[1152,128]{1,0:T(8,128)S(1)}, u32[]{:S(2)}, u32[]{:S(2)}) collective-permute-start(f32[1152,128]{1,0:T(8,128)S(1)} %get-tuple-element.10), channel_id=1, source_target_pairs={{0,2},{2,0},{1,3},{3,1},{4,6},{6,4},{5,7},{7,5},{8,10},{10,8},{9,1... | collective-permute-start | bytes 1769480 | tf_op jit(solution)/shard_map/ppermute | solution.py:289
  69.8 17.8 %all-to-all-start.1 = ((f32[64,1,2304]{2,1,0:T(1,128)}), f32[64,1,2304]{2,1,0:T(1,128)S(1)}, u32[]{:S(2)}, u32[]{:S(2)}) async-start(f32[64,1,2304]{2,1,0:T(1,128)} %bitcast.5), calls=%async_computation.1 | async-start | bytes 1179648 | tf_op jit(solution)/shard_map/all_to_all | solution.py:291
  98.9 4.6 %collective-permute-start.1 = (f32[544,128]{1,0:T(8,128)S(1)}, f32[544,128]{1,0:T(8,128)S(1)}, u32[]{:S(2)}, u32[]{:S(2)}) collective-permute-start(f32[544,128]{1,0:T(8,128)S(1)} %bitcast.14), channel_id=1, source_target_pairs={{0,2},{2,0},{1,3},{3,1},{4,6},{6,4},{5,7},{7,5},{8,10},{10,8},{9,1... | collective-permute-start | bytes 835592 | tf_op jit(solution)/shard_map/ppermute | solution.py:313

commit v3 on v2

--- a/solution.py
+++ b/solution.py
@@ -27,35 +27,52 @@
     return jnp.dot(a, b, preferred_element_type=jnp.float32)
 
 
-def pack_kernel(lists, v_ref, ids_ref, codes_ref, out_ref, sem):
+def pack_kernel(lists, v_ref, ids_ref, codes_ref, out_ref, ids_v, codes_v, aux_v, sems):
     rows, dims = v_ref.shape
     subs = codes_ref.shape[0]
-    copy = pltpu.make_async_copy(v_ref, out_ref.at[:, :dims], sem)
-    copy.start()
-    ids = lax.rem(ids_ref[...], lists)
+    moves = [
+        pltpu.make_async_copy(codes_ref, codes_v, sems.at[0]),
+        pltpu.make_async_copy(ids_ref, ids_v, sems.at[1]),
+        pltpu.make_async_copy(v_ref, out_ref.at[:, :dims], sems.at[2]),
+    ]
+    for move in moves:
+        move.start()
+    moves[0].wait()
+    moves[1].wait()
+    ids = lax.rem(ids_v[...], lists)
     high = lax.div(ids, 256)
     aux = jnp.concatenate(
         [
-            codes_ref[...].astype(jnp.float32),
+            codes_v[...].astype(jnp.float32),
             high.astype(jnp.float32),
             (ids - 256 * high).astype(jnp.float32),
             jnp.zeros((LANES - subs - 2, rows), jnp.float32),
         ],
         axis=0,
     )
-    out_ref[:, dims:] = jnp.transpose(aux).astype(jnp.bfloat16)
-    copy.wait()
+    aux_v[...] = jnp.transpose(aux).astype(jnp.bfloat16)
+    last = pltpu.make_async_copy(aux_v, out_ref.at[:, dims:], sems.at[3])
+    last.start()
+    moves[2].wait()
+    last.wait()
 
 
 def pack(vectors, list_ids, codes, lists):
     rows, dims = vectors.shape
+    subs = codes.shape[1]
+    anywhere = pl.BlockSpec(memory_space=pl.ANY)
     return pl.pallas_call(
         functools.partial(pack_kernel, lists),
-        in_specs=[pl.BlockSpec(memory_space=pl.ANY), IN_VMEM, IN_VMEM],
-        out_specs=IN_VMEM,
+        in_specs=[anywhere, anywhere, anywhere],
+        out_specs=anywhere,
         out_shape=jax.ShapeDtypeStruct((rows, dims + LANES), jnp.bfloat16),
-        scratch_shapes=[pltpu.SemaphoreType.DMA],
-        compiler_params=pltpu.CompilerParams(vmem_limit_bytes=12 * MIB),
+        scratch_shapes=[
+            pltpu.VMEM((1, rows), jnp.int32),
+            pltpu.VMEM((subs, rows), jnp.int32),
+            pltpu.VMEM((rows, LANES), jnp.bfloat16),
+            pltpu.SemaphoreType.DMA((4,)),
+        ],
+        compiler_params=pltpu.CompilerParams(vmem_limit_bytes=56 * MIB),
         name="pack",
     )(vectors, list_ids.reshape(1, rows), jnp.transpose(codes))
 
@@ -81,7 +98,9 @@
     extra,
     ids_v,
     ids_s,
+    nc_v,
     sem,
+    nc_sem,
 ):
     rows = arr_ref.shape[0]
     lists, dims = cent_ref.shape
@@ -113,8 +132,10 @@
             at = slice(tile * LANES, (tile + 1) * LANES)
             old = cent_ref[:, at].astype(jnp.float32)
             nc = (totals[:, h * LANES : (h + 1) * LANES] + prior * old) * inv[...]
-            nc_ref[:, at] = nc
+            nc_v[:, at] = nc
             table[pl.ds(tile, lists, stride=tiles), :] = nc
+    nc_copy = pltpu.make_async_copy(nc_v, nc_ref, nc_sem)
+    nc_copy.start()
     copy.wait()
 
     def pick(q, _):
@@ -199,6 +220,7 @@
         return 0
 
     lax.fori_loop(0, dims // COLS, columns, 0)
+    nc_copy.wait()
 
 
 def local_pass(core, arrived, centroids, subs, width, prior, parts):
@@ -210,7 +232,7 @@
     return pl.pallas_call(
         functools.partial(local_kernel, subs, width, parts, prior, 256),
         in_specs=[pl.BlockSpec(memory_space=pltpu.SMEM), IN_VMEM, IN_VMEM],
-        out_specs=[IN_VMEM, IN_VMEM, IN_VMEM],
+        out_specs=[pl.BlockSpec(memory_space=pl.ANY), IN_VMEM, IN_VMEM],
         out_shape=[jax.ShapeDtypeStruct((lists, dims), jnp.float32), sums, sums],
         scratch_shapes=[
             pltpu.VMEM((lists, rows), jnp.bfloat16),
@@ -222,6 +244,8 @@
             pltpu.VMEM((rows, LANES), jnp.bfloat16),
             pltpu.VMEM((1, rows), jnp.int32),
             pltpu.SMEM((1, rows), jnp.int32),
+            pltpu.VMEM((lists, dims), jnp.float32),
+            pltpu.SemaphoreType.DMA,
             pltpu.SemaphoreType.DMA,
         ],
         compiler_params=pltpu.CompilerParams(vmem_limit_bytes=32 * MIB),

time: 105 us -> 164 us (1.56)
  Pallas kernels: 16.2 us -> 80.5 us
  local copies, waits for them, and re-layouts: 5.93 us -> 1.24 us
    pallas_call x1, Pallas kernels: 0.42 us -> 64.7 us  [pack(): pl.pallas_call(functools.partial(pack_kernel, lists), in_specs=[anywhere,...]
    unnamed x12 -> x4, local copies, waits for them, and re-layouts: 5.92 us -> 1.23 us
where the time goes in v3:
time: 164 us
  Pallas kernels  80.5 us (49%)
  waiting for transfers between devices  48.1 us (29%)
  starting transfers between devices  21.4 us (13%)
  blocking collectives  11.2 us (7%)
    pallas_call x1, Pallas kernels, pack(): pl.pallas_call(functools.partial(pack_kernel, lists), in_specs=[anywhere,...  64.7 us
    all_to_all x1, waiting for transfers between devices, on_device(): lax.all_to_all(sent, SPLIT, split_axis=0, concat_axis=0, tiled=True)  32.3 us
    pallas_call x1, Pallas kernels, local_pass(): pl.pallas_call(functools.partial(local_kernel, subs, width, parts, prior,...  14.8 us
    all_to_all x1, waiting for transfers between devices, on_device(): lax.all_to_all(paired.reshape(chips * parts, 1, held * LANES), ('chip', '...  12.9 us
    all_to_all x1, starting transfers between devices, on_device(): lax.all_to_all(sent, SPLIT, split_axis=0, concat_axis=0, tiled=True)  11.5 us
    all_to_all x1, blocking collectives, on_device(): lax.all_to_all(done.reshape(chips, 1, held * LANES), 'chip', split_axis=0...  11.2 us
    all_to_all x1, starting transfers between devices, on_device(): lax.all_to_all(paired.reshape(chips * parts, 1, held * LANES), ('chip', '...  4.86 us
    ppermute x1, starting transfers between devices, on_device(): other = lax.ppermute(half, 'core', swap)  3.43 us
  transfers between devices with their start and end apart: 4, of which 4 were waited for; matrix products, arithmetic and copies ran while one was open for 0% of the time, Pallas kernels for 0%

profile of v3, /device:TPU:1, one launch (start us, length us, event | category | flops | bytes accessed | tf_op | source)
XLA Modules:
  0.0 163.9 jit_solution(7189193085847492798)
XLA Ops:
  0.6 0.0 copy-start
  0.6 64.7 %pack.1 = bf16[1024,1152]{1,0:T(8,128)(2,1)} custom-call(bf16[1024,1024]{1,0:T(8,128)(2,1)} %v_ref.1, s32[1,1024]{1,0:T(1,128)} %bitcast.18, s32[64,1024]{1,0:T(8,128)} %bitcast.17), custom_call_target="tpu_custom_call" | custom-call | tf_op jit(solution)/shard_map/pack/pallas_call | solution.py:64
  65.3 11.5 %all-to-all-start = ((bf16[128,8,1152]{2,1,0:T(8,128)(2,1)}), bf16[128,8,1152]{2,1,0:T(8,128)(2,1)S(1)}, u32[]{:S(2)}, u32[]{:S(2)}) async-start(bf16[128,8,1152]{2,1,0:T(8,128)(2,1)} %bitcast.16), calls=%async_computation | async-start | bytes 4718592 | tf_op jit(solution)/shard_map/all_to_all | solution.py:309
  76.8 32.3 %all-to-all-done = bf16[128,8,1152]{2,1,0:T(8,128)(2,1)S(1)} async-done(((bf16[128,8,1152]{2,1,0:T(8,128)(2,1)}), bf16[128,8,1152]{2,1,0:T(8,128)(2,1)S(1)}, u32[]{:S(2)}, u32[]{:S(2)}) %all-to-all-start) | async-done | bytes 2359328 | tf_op jit(solution)/shard_map/all_to_all | solution.py:309
  109.2 0.0 copy-start.1
  109.2 1.2 copy-done.1
  110.4 14.8 %local_pass.1 = (f32[512,1024]{1,0:T(8,128)}, f32[1152,128]{1,0:T(8,128)S(1)}, f32[1152,128]{1,0:T(8,128)S(1)}) custom-call(s32[1]{0:T(128)} %bitcast.core_ref, bf16[1024,1152]{1,0:T(8,128)(2,1)S(1)} %bitcast.11, bf16[512,1024]{1,0:T(8,128)(2,1)S(1)} %copy-done.1), custom_call_target="tpu_custom_call" | custom-call | tf_op jit(solution)/shard_map/local_pass/pallas_call | solution.py:232
  125.2 1.6 collective-permute-start
  126.8 1.6 collective-permute-done
  128.4 0.9 add.9
  129.3 4.9 %all-to-all-start.1 = ((f32[64,1,2304]{2,1,0:T(1,128)}), f32[64,1,2304]{2,1,0:T(1,128)S(1)}, u32[]{:S(2)}, u32[]{:S(2)}) async-start(f32[64,1,2304]{2,1,0:T(1,128)} %bitcast.5), calls=%async_computation.1 | async-start | bytes 1179648 | tf_op jit(solution)/shard_map/all_to_all | solution.py:315
  134.2 0.0 copy-done
  134.2 12.9 %all-to-all-done.1 = f32[64,1,2304]{2,1,0:T(1,128)S(1)} async-done(((f32[64,1,2304]{2,1,0:T(1,128)}), f32[64,1,2304]{2,1,0:T(1,128)S(1)}, u32[]{:S(2)}, u32[]{:S(2)}) %all-to-all-start.1) | async-done | bytes 589856 | tf_op jit(solution)/shard_map/all_to_all | solution.py:315
  147.1 0.2 owner_pass.1
  147.3 11.2 %all_to_all.21 = f32[32,1,2176]{2,1,0:T(1,128)S(1)} all-to-all(f32[32,1,2176]{2,1,0:T(1,128)S(1)} %bitcast.15), channel_id=1, replica_groups=mesh['chip'=32,'core'=2,'sub'=2] {'chip'}, dimensions={0} | all-to-all | bytes 557056 | tf_op jit(solution)/shard_map/all_to_all | solution.py:334
  158.5 3.4 %collective-permute-start.1 = (f32[544,128]{1,0:T(8,128)S(1)}, f32[544,128]{1,0:T(8,128)S(1)}, u32[]{:S(2)}, u32[]{:S(2)}) collective-permute-start(f32[544,128]{1,0:T(8,128)S(1)} %bitcast.13), channel_id=1, source_target_pairs={{0,2},{2,0},{1,3},{3,1},{4,6},{6,4},{5,7},{7,5},{8,10},{10,8},{9,1... | collective-permute-start | bytes 835592 | tf_op jit(solution)/shard_map/ppermute | solution.py:337
  161.9 1.2 collective-permute-done.1.other_ref
  163.1 0.8 finish.1
  (1 shorter events, 0.0 us)
Async XLA Ops:
  0.6 133.6 %copy-start = (f32[32,16,256]{2,1,0:T(8,128)S(1)}, f32[32,16,256]{2,1,0:T(8,128)}, u32[]{:S(2)}) copy-start(f32[32,16,256]{2,1,0:T(8,128)} %param.9) | copy-start | bytes 1572868
  65.3 43.8 %all-to-all-start = ((bf16[128,8,1152]{2,1,0:T(8,128)(2,1)}), bf16[128,8,1152]{2,1,0:T(8,128)(2,1)S(1)}, u32[]{:S(2)}, u32[]{:S(2)}) async-start(bf16[128,8,1152]{2,1,0:T(8,128)(2,1)} %bitcast.16), calls=%async_computation | async-start | bytes 4718592 | tf_op jit(solution)/shard_map/all_to_all | solution.py:309
  109.2 1.2 copy-start.1
  125.2 3.3 %collective-permute-start = (f32[1152,128]{1,0:T(8,128)S(1)}, f32[1152,128]{1,0:T(8,128)S(1)}, u32[]{:S(2)}, u32[]{:S(2)}) collective-permute-start(f32[1152,128]{1,0:T(8,128)S(1)} %get-tuple-element.10), channel_id=1, source_target_pairs={{0,2},{2,0},{1,3},{3,1},{4,6},{6,4},{5,7},{7,5},{8,10},{10,8},{9,1... | collective-permute-start | bytes 1769480 | tf_op jit(solution)/shard_map/ppermute | solution.py:313
  129.3 17.8 %all-to-all-start.1 = ((f32[64,1,2304]{2,1,0:T(1,128)}), f32[64,1,2304]{2,1,0:T(1,128)S(1)}, u32[]{:S(2)}, u32[]{:S(2)}) async-start(f32[64,1,2304]{2,1,0:T(1,128)} %bitcast.5), calls=%async_computation.1 | async-start | bytes 1179648 | tf_op jit(solution)/shard_map/all_to_all | solution.py:315
  158.5 4.6 %collective-permute-start.1 = (f32[544,128]{1,0:T(8,128)S(1)}, f32[544,128]{1,0:T(8,128)S(1)}, u32[]{:S(2)}, u32[]{:S(2)}) collective-permute-start(f32[544,128]{1,0:T(8,128)S(1)} %bitcast.13), channel_id=1, source_target_pairs={{0,2},{2,0},{1,3},{3,1},{4,6},{6,4},{5,7},{7,5},{8,10},{10,8},{9,1... | collective-permute-start | bytes 835592 | tf_op jit(solution)/shard_map/ppermute | solution.py:337

commit v4 on v3

--- a/solution.py
+++ b/solution.py
@@ -27,18 +27,28 @@
     return jnp.dot(a, b, preferred_element_type=jnp.float32)
 
 
-def pack_kernel(lists, v_ref, ids_ref, codes_ref, out_ref, ids_v, codes_v, aux_v, sems):
+def pack_kernel(
+    lists, pieces, v_ref, ids_ref, codes_ref, out_ref, held, ids_v, codes_v, ins, outs
+):
     rows, dims = v_ref.shape
     subs = codes_ref.shape[0]
+    step = rows // pieces
+    first = [
+        pltpu.make_async_copy(codes_ref, codes_v, ins.at[pieces]),
+        pltpu.make_async_copy(ids_ref, ids_v, ins.at[pieces + 1]),
+    ]
     moves = [
-        pltpu.make_async_copy(codes_ref, codes_v, sems.at[0]),
-        pltpu.make_async_copy(ids_ref, ids_v, sems.at[1]),
-        pltpu.make_async_copy(v_ref, out_ref.at[:, :dims], sems.at[2]),
+        pltpu.make_async_copy(
+            v_ref.at[pl.ds(i * step, step)],
+            held.at[pl.ds(i * step, step), pl.ds(0, dims)],
+            ins.at[i],
+        )
+        for i in range(pieces)
     ]
-    for move in moves:
+    for move in first + moves:
         move.start()
-    moves[0].wait()
-    moves[1].wait()
+    for move in first:
+        move.wait()
     ids = lax.rem(ids_v[...], lists)
     high = lax.div(ids, 256)
     aux = jnp.concatenate(
@@ -50,29 +60,36 @@
         ],
         axis=0,
     )
-    aux_v[...] = jnp.transpose(aux).astype(jnp.bfloat16)
-    last = pltpu.make_async_copy(aux_v, out_ref.at[:, dims:], sems.at[3])
-    last.start()
-    moves[2].wait()
-    last.wait()
+    held[:, dims:] = jnp.transpose(aux).astype(jnp.bfloat16)
+    sends = []
+    for i, move in enumerate(moves):
+        move.wait()
+        at = pl.ds(i * step, step)
+        send = pltpu.make_async_copy(held.at[at], out_ref.at[at], outs.at[i])
+        send.start()
+        sends.append(send)
+    for send in sends:
+        send.wait()
 
 
 def pack(vectors, list_ids, codes, lists):
     rows, dims = vectors.shape
     subs = codes.shape[1]
+    pieces = 8
     anywhere = pl.BlockSpec(memory_space=pl.ANY)
     return pl.pallas_call(
-        functools.partial(pack_kernel, lists),
-        in_specs=[anywhere, anywhere, anywhere],
+        functools.partial(pack_kernel, lists, pieces),
+        in_specs=[anywhere] * 3,
         out_specs=anywhere,
         out_shape=jax.ShapeDtypeStruct((rows, dims + LANES), jnp.bfloat16),
         scratch_shapes=[
+            pltpu.VMEM((rows, dims + LANES), jnp.bfloat16),
             pltpu.VMEM((1, rows), jnp.int32),
             pltpu.VMEM((subs, rows), jnp.int32),
-            pltpu.VMEM((rows, LANES), jnp.bfloat16),
-            pltpu.SemaphoreType.DMA((4,)),
-        ],
-        compiler_params=pltpu.CompilerParams(vmem_limit_bytes=56 * MIB),
+            pltpu.SemaphoreType.DMA((pieces + 2,)),
+            pltpu.SemaphoreType.DMA((pieces,)),
+        ],
+        compiler_params=pltpu.CompilerParams(vmem_limit_bytes=58 * MIB),
         name="pack",
     )(vectors, list_ids.reshape(1, rows), jnp.transpose(codes))
 
@@ -130,8 +147,8 @@
         for h in range(side):
             tile = j * side + h
             at = slice(tile * LANES, (tile + 1) * LANES)
-            old = cent_ref[:, at].astype(jnp.float32)
-            nc = (totals[:, h * LANES : (h + 1) * LANES] + prior * old) * inv[...]
+            old = prior * cent_ref[:, at].astype(jnp.float32)
+            nc = (totals[:, h * LANES : (h + 1) * LANES] + old) * inv[...]
             nc_v[:, at] = nc
             table[pl.ds(tile, lists, stride=tiles), :] = nc
     nc_copy = pltpu.make_async_copy(nc_v, nc_ref, nc_sem)
@@ -231,7 +248,11 @@
     sums = jax.ShapeDtypeStruct((subs * (width + 2), LANES), jnp.float32)
     return pl.pallas_call(
         functools.partial(local_kernel, subs, width, parts, prior, 256),
-        in_specs=[pl.BlockSpec(memory_space=pltpu.SMEM), IN_VMEM, IN_VMEM],
+        in_specs=[
+            pl.BlockSpec(memory_space=pltpu.SMEM),
+            IN_VMEM,
+            IN_VMEM,
+        ],
         out_specs=[pl.BlockSpec(memory_space=pl.ANY), IN_VMEM, IN_VMEM],
         out_shape=[jax.ShapeDtypeStruct((lists, dims), jnp.float32), sums, sums],
         scratch_shapes=[
@@ -305,7 +326,7 @@
     core_arg = core.astype(jnp.int32).reshape(1)
     swap = [(0, 1), (1, 0)]
 
-    sent = pack(vectors, list_ids, codes, lists)
+    sent, core_arg = lax.optimization_barrier((pack(vectors, list_ids, codes, lists), core_arg))
     arrived = lax.all_to_all(sent, SPLIT, split_axis=0, concat_axis=0, tiled=True)
     new_centroids, keep, give = local_pass(
         core_arg, arrived, centroids, subs, width, prior_lists, parts

time: 164 us -> 101 us (0.62)
  Pallas kernels: 80.5 us -> 18.5 us
  blocking collectives: 11.2 us -> 55 us
  waiting for transfers between devices: 48.1 us -> 15.7 us
  starting transfers between devices: 21.4 us -> 9.91 us
    pallas_call x1, Pallas kernels: 64.7 us -> 2.71 us  [pack(): pl.pallas_call(functools.partial(pack_kernel, lists, pieces), in_specs=[a...]
    all_to_all x0 -> x1, blocking collectives: none -> 43.8 us  [on_device(): lax.all_to_all(sent, SPLIT, split_axis=0, concat_axis=0, tiled=True)]
    all_to_all x1 -> x0, waiting for transfers between devices: 32.3 us -> none  [on_device(): lax.all_to_all(sent, SPLIT, split_axis=0, concat_axis=0, tiled=True)]
    all_to_all x1 -> x0, starting transfers between devices: 11.5 us -> none  [on_device(): lax.all_to_all(sent, SPLIT, split_axis=0, concat_axis=0, tiled=True)]
  transfers between devices with their start and end apart: 4 -> 3, of which waited for: 4 -> 3; matrix products, arithmetic and copies ran while one was open for 0% -> 0% of each run, Pallas kernels for 0% -> 0%
where the time goes in v4:
time: 101 us
  blocking collectives  55 us (54%)
  Pallas kernels  18.5 us (18%)
  waiting for transfers between devices  15.7 us (16%)
  starting transfers between devices  9.91 us (10%)
    all_to_all x1, blocking collectives, on_device(): lax.all_to_all(sent, SPLIT, split_axis=0, concat_axis=0, tiled=True)  43.8 us
    pallas_call x1, Pallas kernels, local_pass(): pl.pallas_call(functools.partial(local_kernel, subs, width, parts, prior,...  14.8 us
    all_to_all x1, waiting for transfers between devices, on_device(): lax.all_to_all(paired.reshape(chips * parts, 1, held * LANES), ('chip', '...  12.9 us
    all_to_all x1, blocking collectives, on_device(): lax.all_to_all(done.reshape(chips, 1, held * LANES), 'chip', split_axis=0...  11.2 us
    all_to_all x1, starting transfers between devices, on_device(): lax.all_to_all(paired.reshape(chips * parts, 1, held * LANES), ('chip', '...  4.86 us
    ppermute x1, starting transfers between devices, on_device(): other = lax.ppermute(half, 'core', swap)  3.43 us
    pallas_call x1, Pallas kernels, pack(): pl.pallas_call(functools.partial(pack_kernel, lists, pieces), in_specs=[a...  2.71 us
  transfers between devices with their start and end apart: 3, of which 3 were waited for; matrix products, arithmetic and copies ran while one was open for 0% of the time, Pallas kernels for 0%

profile of v4, /device:TPU:1, one launch (start us, length us, event | category | flops | bytes accessed | tf_op | source)
XLA Modules:
  0.0 100.8 jit_solution(11641351202658391157)
XLA Ops:
  0.6 0.0 copy-start
  0.7 2.7 %pack.1 = bf16[1024,1152]{1,0:T(8,128)(2,1)} custom-call(bf16[1024,1024]{1,0:T(8,128)(2,1)} %v_ref.1, s32[1,1024]{1,0:T(1,128)} %bitcast.18, s32[64,1024]{1,0:T(8,128)} %bitcast.17), custom_call_target="tpu_custom_call" | custom-call | tf_op jit(solution)/shard_map/pack/pallas_call | solution.py:80
  3.4 0.0 copy-start.1
  3.4 43.8 %all_to_all.21 = bf16[128,8,1152]{2,1,0:T(8,128)(2,1)S(1)} all-to-all(bf16[128,8,1152]{2,1,0:T(8,128)(2,1)} %bitcast.16), channel_id=1, replica_groups=mesh['chip'=32,'core'=2,'sub'=2] {'chip','core','sub'}, dimensions={0} | all-to-all | bytes 4718592 | tf_op jit(solution)/shard_map/all_to_all | solution.py:330
  47.2 0.0 copy-done.1
  47.2 14.8 %local_pass.1 = (f32[512,1024]{1,0:T(8,128)}, f32[1152,128]{1,0:T(8,128)S(1)}, f32[1152,128]{1,0:T(8,128)S(1)}) custom-call(s32[1]{0:T(128)} %bitcast.2.core_ref, bf16[1024,1152]{1,0:T(8,128)(2,1)S(1)} %bitcast.11, bf16[512,1024]{1,0:T(8,128)(2,1)S(1)} %copy-done.1), custom_call_target="tpu_custom_call" | custom-call | tf_op jit(solution)/shard_map/local_pass/pallas_call | solution.py:249
  62.0 1.6 %collective-permute-start = (f32[1152,128]{1,0:T(8,128)S(1)}, f32[1152,128]{1,0:T(8,128)S(1)}, u32[]{:S(2)}, u32[]{:S(2)}) collective-permute-start(f32[1152,128]{1,0:T(8,128)S(1)} %get-tuple-element.14), channel_id=1, source_target_pairs={{0,2},{2,0},{1,3},{3,1},{4,6},{6,4},{5,7},{7,5},{8,10},{10,8},{9,1... | collective-permute-start | bytes 1769480 | tf_op jit(solution)/shard_map/ppermute | solution.py:334
  63.7 1.6 %collective-permute-done = f32[1152,128]{1,0:T(8,128)S(1)} collective-permute-done((f32[1152,128]{1,0:T(8,128)S(1)}, f32[1152,128]{1,0:T(8,128)S(1)}, u32[]{:S(2)}, u32[]{:S(2)}) %collective-permute-start) | collective-permute-done | bytes 589856 | tf_op jit(solution)/shard_map/ppermute | solution.py:334
  65.3 0.9 add.9
  66.2 4.9 %all-to-all-start.1 = ((f32[64,1,2304]{2,1,0:T(1,128)}), f32[64,1,2304]{2,1,0:T(1,128)S(1)}, u32[]{:S(2)}, u32[]{:S(2)}) async-start(f32[64,1,2304]{2,1,0:T(1,128)} %bitcast.5), calls=%async_computation.1 | async-start | bytes 1179648 | tf_op jit(solution)/shard_map/all_to_all | solution.py:336
  71.0 0.0 copy-done
  71.1 12.9 %all-to-all-done.1 = f32[64,1,2304]{2,1,0:T(1,128)S(1)} async-done(((f32[64,1,2304]{2,1,0:T(1,128)}), f32[64,1,2304]{2,1,0:T(1,128)S(1)}, u32[]{:S(2)}, u32[]{:S(2)}) %all-to-all-start.1) | async-done | bytes 589856 | tf_op jit(solution)/shard_map/all_to_all | solution.py:336
  84.0 0.2 owner_pass.1
  84.2 11.2 %all_to_all.22 = f32[32,1,2176]{2,1,0:T(1,128)S(1)} all-to-all(f32[32,1,2176]{2,1,0:T(1,128)S(1)} %bitcast.15), channel_id=1, replica_groups=mesh['chip'=32,'core'=2,'sub'=2] {'chip'}, dimensions={0} | all-to-all | bytes 557056 | tf_op jit(solution)/shard_map/all_to_all | solution.py:355
  95.3 3.4 %collective-permute-start.1 = (f32[544,128]{1,0:T(8,128)S(1)}, f32[544,128]{1,0:T(8,128)S(1)}, u32[]{:S(2)}, u32[]{:S(2)}) collective-permute-start(f32[544,128]{1,0:T(8,128)S(1)} %bitcast.13), channel_id=1, source_target_pairs={{0,2},{2,0},{1,3},{3,1},{4,6},{6,4},{5,7},{7,5},{8,10},{10,8},{9,1... | collective-permute-start | bytes 835592 | tf_op jit(solution)/shard_map/ppermute | solution.py:358
  98.8 1.2 %collective-permute-done.1.other_ref = f32[544,128]{1,0:T(8,128)S(1)} collective-permute-done((f32[544,128]{1,0:T(8,128)S(1)}, f32[544,128]{1,0:T(8,128)S(1)}, u32[]{:S(2)}, u32[]{:S(2)}) %collective-permute-start.1) | collective-permute-done | bytes 278560 | tf_op jit(solution)/shard_map/ppermute | solution.py:358
  100.0 0.8 finish.1
  (1 shorter events, 0.0 us)
Async XLA Ops:
  0.6 70.4 %copy-start = (f32[32,16,256]{2,1,0:T(8,128)S(1)}, f32[32,16,256]{2,1,0:T(8,128)}, u32[]{:S(2)}) copy-start(f32[32,16,256]{2,1,0:T(8,128)} %param.9) | copy-start | bytes 1572868
  3.4 43.9 %copy-start.1 = (bf16[512,1024]{1,0:T(8,128)(2,1)S(1)}, bf16[512,1024]{1,0:T(8,128)(2,1)}, u32[]{:S(2)}) copy-start(bf16[512,1024]{1,0:T(8,128)(2,1)} %cent_ref.1) | copy-start | bytes 3145732
  62.0 3.3 %collective-permute-start = (f32[1152,128]{1,0:T(8,128)S(1)}, f32[1152,128]{1,0:T(8,128)S(1)}, u32[]{:S(2)}, u32[]{:S(2)}) collective-permute-start(f32[1152,128]{1,0:T(8,128)S(1)} %get-tuple-element.14), channel_id=1, source_target_pairs={{0,2},{2,0},{1,3},{3,1},{4,6},{6,4},{5,7},{7,5},{8,10},{10,8},{9,1... | collective-permute-start | bytes 1769480 | tf_op jit(solution)/shard_map/ppermute | solution.py:334
  66.2 17.8 %all-to-all-start.1 = ((f32[64,1,2304]{2,1,0:T(1,128)}), f32[64,1,2304]{2,1,0:T(1,128)S(1)}, u32[]{:S(2)}, u32[]{:S(2)}) async-start(f32[64,1,2304]{2,1,0:T(1,128)} %bitcast.5), calls=%async_computation.1 | async-start | bytes 1179648 | tf_op jit(solution)/shard_map/all_to_all | solution.py:336
  95.3 4.6 %collective-permute-start.1 = (f32[544,128]{1,0:T(8,128)S(1)}, f32[544,128]{1,0:T(8,128)S(1)}, u32[]{:S(2)}, u32[]{:S(2)}) collective-permute-start(f32[544,128]{1,0:T(8,128)S(1)} %bitcast.13), channel_id=1, source_target_pairs={{0,2},{2,0},{1,3},{3,1},{4,6},{6,4},{5,7},{7,5},{8,10},{10,8},{9,1... | collective-permute-start | bytes 835592 | tf_op jit(solution)/shard_map/ppermute | solution.py:358

commit v5 on v4

--- a/solution.py
+++ b/solution.py
@@ -111,7 +111,10 @@
     code_t,
     table,
     picked,
-    resid,
+    low_v,
+    high_v,
+    norms,
+    side_v,
     extra,
     ids_v,
     ids_s,
@@ -121,16 +124,17 @@
 ):
     rows = arr_ref.shape[0]
     lists, dims = cent_ref.shape
-    levels = 2 * LANES
+    tiles = dims // LANES
     here = COLS // width
     group = LANES // width
-    tiles = dims // LANES
     side = COLS // LANES
     held = width + 2
+    quad = group // 2
+    kinds = 4
     first_core = core_ref[0] == 0
 
-    aux = arr_ref[:, dims:].astype(jnp.float32)
-    aux_t = jnp.transpose(aux)
+    aux = arr_ref[:, dims:]
+    aux_t = jnp.transpose(aux.astype(jnp.float32))
     row_ids = (aux_t[subs : subs + 1] * 256.0 + aux_t[subs + 1 : subs + 2]).astype(jnp.int32)
     ids_v[...] = row_ids * tiles
     copy = pltpu.make_async_copy(ids_v, ids_s, sem)
@@ -139,8 +143,16 @@
     hot[...] = jnp.where(level == row_ids, 1.0, 0.0).astype(jnp.bfloat16)
     counts = dot(hot[...], jnp.ones((rows, LANES), jnp.bfloat16))
     inv[...] = 1.0 / (counts + prior)
-    for b in range(subs // here):
-        code_t[b] = aux_t[b * here : (b + 1) * here].astype(jnp.int32)
+    for b in range(subs // group):
+        block = aux_t[b * group : (b + 1) * group].astype(jnp.int32)
+        code_t[b] = jnp.where(block < LANES, block, block - LANES)
+    line = lax.broadcasted_iota(jnp.int32, (LANES, LANES), 0)
+    lane = lax.broadcasted_iota(jnp.int32, (LANES, LANES), 1)
+    twice = jnp.where(line == lax.rem(lane, subs), 1.0, 0.0).astype(jnp.bfloat16)
+    both = dot(aux, twice)
+    lane = lax.broadcasted_iota(jnp.int32, (rows, LANES), 1)
+    inside = jnp.where((both < LANES) == (lane < subs), 1.0, 0.0)
+    side_v[:, 3 * LANES :] = inside.astype(jnp.bfloat16)
 
     for j in range(dims // COLS):
         totals = dot(hot[...], arr_ref[:, j * COLS : (j + 1) * COLS])
@@ -164,14 +176,16 @@
 
     lax.fori_loop(0, rows // 8, pick, 0)
 
-    source = lax.broadcasted_iota(jnp.int32, (COLS, LANES), 0) // width
-    target = lax.broadcasted_iota(jnp.int32, (COLS, LANES), 1)
-    spread = jnp.where((target % here == source) & (target < 3 * here), 1.0, 0.0).astype(
-        jnp.bfloat16
-    )
-
-    def columns(j, _):
+    def residuals(j, _):
         at = pl.ds(pl.multiple_of(j * COLS, COLS), COLS)
+        line = lax.broadcasted_iota(jnp.int32, (LANES, COLS), 0)
+        column = lax.broadcasted_iota(jnp.int32, (LANES, COLS), 1)
+        widen = jnp.where(line == j * here + column // width, 1.0, 0.0).astype(jnp.bfloat16)
+        line = lax.broadcasted_iota(jnp.int32, (COLS, LANES), 0)
+        column = lax.broadcasted_iota(jnp.int32, (COLS, LANES), 1)
+        fold = jnp.where(
+            lax.rem(column, subs) == j * here + line // width, 1.0, 0.0
+        ).astype(jnp.bfloat16)
         for i in range(rows // chunk):
             ra = slice(i * chunk, (i + 1) * chunk)
             near = jnp.concatenate(
@@ -182,61 +196,104 @@
                 axis=1,
             )
             r = (arr_ref[ra, at].astype(jnp.float32) - near).astype(jnp.bfloat16)
-            resid[ra, :] = r
             wide = r.astype(jnp.float32)
+            low = r * dot(side_v[ra, 3 * LANES :], widen).astype(jnp.bfloat16)
+            low_v[ra, at] = low
+            high_v[ra, at] = r - low
             square = wide * wide
             square_hi = square.astype(jnp.bfloat16)
             square_lo = (square - square_hi.astype(jnp.float32)).astype(jnp.bfloat16)
-            n_hi, n_mid, n_lo = split3(dot(square_hi, spread) + dot(square_lo, spread))
-            lane = lax.broadcasted_iota(jnp.int32, (chunk, LANES), 1)
-            extra[ra, :] = jnp.where(
-                lane < here,
-                n_hi.astype(jnp.float32),
-                jnp.where(
-                    lane < 2 * here,
-                    n_mid.astype(jnp.float32),
-                    jnp.where(lane < 3 * here, n_lo.astype(jnp.float32), 1.0),
-                ),
-            ).astype(jnp.bfloat16)
-
-        codes = code_t[j]
-        level = lax.broadcasted_iota(jnp.int32, (levels, rows), 0)
-        lane = lax.broadcasted_iota(jnp.int32, (levels, LANES), 1)
-        extra_sum = jnp.zeros((levels, LANES), jnp.float32)
-        pieces = []
+            found = dot(square_hi, fold) + dot(square_lo, fold)
+            norms[ra, :] = jnp.where(j == 0, found, norms[ra, :] + found)
+        return 0
+
+    lax.fori_loop(0, dims // COLS, residuals, 0)
+
+    for i in range(rows // chunk):
+        ra = slice(i * chunk, (i + 1) * chunk)
+        pieces = split3(norms[ra, :] * side_v[ra, 3 * LANES :].astype(jnp.float32))
+        for k, piece in enumerate(pieces):
+            side_v[ra, k * LANES : (k + 1) * LANES] = piece
+
+    def columns(j, _):
+        line = lax.broadcasted_iota(jnp.int32, (kinds * LANES, COLS), 0)
+        column = lax.broadcasted_iota(jnp.int32, (kinds * LANES, COLS), 1)
+        spot = lax.rem(column, LANES // 2)
+        in_first = lax.rem(column, LANES) >= LANES // 2
+        kind = spot // (2 * quad)
+        half = lax.rem(spot, 2 * quad) // quad
+        sub = (
+            j * here
+            + (column // LANES) * group
+            + jnp.where(in_first, 0, quad)
+            + lax.rem(spot, quad)
+        )
+        wanted = kind * LANES + half * subs + sub
+        move = jnp.where((line == wanted) & (kind < kinds), 1.0, 0.0).astype(jnp.bfloat16)
+        for i in range(rows // chunk):
+            ra = slice(i * chunk, (i + 1) * chunk)
+            extra[ra, :] = dot(side_v[ra, :], move).astype(jnp.bfloat16)
+
+        level = lax.broadcasted_iota(jnp.int32, (LANES, rows), 0)
+        lane = lax.broadcasted_iota(jnp.int32, (LANES, LANES), 1)
+        wide_lane = lax.broadcasted_iota(jnp.int32, (rows, LANES), 1)
+        steps = subs // parts // here
         for part in range(side):
-            weights = jnp.concatenate(
-                [resid[:, part * LANES : (part + 1) * LANES], extra[...]], axis=1
-            )
-            sums = jnp.zeros((levels, LANES), jnp.float32)
-            for k in range(group):
-                i = part * group + k
-                onehot = jnp.where(level == codes[i : i + 1], 1.0, 0.0).astype(jnp.bfloat16)
-                found = dot(onehot, weights)
-                sums = jnp.where(lane // width == k, found[:, :LANES], sums)
-                extra_sum = jnp.where(lane % here == i, found[:, LANES:], extra_sum)
-            pieces.append(jnp.transpose(sums))
-        tail = jnp.transpose(extra_sum)
-        norm_sum = (tail[:here] + tail[here : 2 * here]) + tail[2 * here : 3 * here]
-        count_sum = tail[3 * here : 4 * here]
-        steps = subs // parts // here
-        for i in range(here):
-            part, k = divmod(i, group)
-            block = jnp.concatenate(
-                [
-                    pieces[part][k * width : (k + 1) * width],
-                    count_sum[i : i + 1],
-                    norm_sum[i : i + 1],
-                ],
-                axis=0,
-            )
-            left, right = block[:, :LANES], block[:, LANES:]
-            at_row = ((lax.rem(j, steps) * here + i) * parts + lax.div(j, steps)) * held
-            keep_ref[pl.ds(at_row, held), :] = jnp.where(first_core, left, right)
-            give_ref[pl.ds(at_row, held), :] = jnp.where(first_core, right, left)
+            at = pl.ds(pl.multiple_of(j * COLS + part * LANES, LANES), LANES)
+            codes = code_t[j * side + part]
+            codes16 = codes.astype(jnp.float32).astype(jnp.bfloat16)
+            level16 = level.astype(jnp.float32).astype(jnp.bfloat16)
+            beside = extra[:, part * LANES : (part + 1) * LANES]
+            low_sum = jnp.zeros((LANES, LANES), jnp.float32)
+            high_sum = low_sum
+            extra_sum = low_sum
+            for q in range(2):
+                own = (wide_lane < LANES // 2) == (q == 0)
+                mixed = jnp.where(own, high_v[:, at], beside)
+                weights = jnp.concatenate([low_v[:, at], mixed], axis=1)
+                apart = (lane >= LANES // 2) == (q == 0)
+                onehot = jnp.concatenate(
+                    [
+                        jnp.where(level16 == codes16[i : i + 1], jnp.ones((), jnp.bfloat16), jnp.zeros((), jnp.bfloat16))
+                        for i in range(q * quad, (q + 1) * quad)
+                    ],
+                    axis=0,
+                )
+                every = dot(onehot, weights)
+                for k in range(quad):
+                    i = q * quad + k
+                    found = every[k * LANES : (k + 1) * LANES]
+                    low_sum = jnp.where(lane // width == i, found[:, :LANES], low_sum)
+                    high_sum = jnp.where(lane // width == i, found[:, LANES:], high_sum)
+                    extra_sum = jnp.where(
+                        apart & (lax.rem(lane, quad) == k), found[:, LANES:], extra_sum
+                    )
+            low_t = jnp.transpose(low_sum)
+            high_t = jnp.transpose(high_sum)
+            extra_t = jnp.transpose(extra_sum)
+            for i in range(group):
+                q, k = divmod(i, quad)
+                base = LANES // 2 if q == 0 else 0
+                blocks = []
+                for half, sums in ((0, low_t), (1, high_t)):
+                    found = [
+                        extra_t[row : row + 1]
+                        for row in range(base + half * quad + k, base + LANES // 2, 2 * quad)
+                    ]
+                    norm = (found[0] + found[1]) + found[2]
+                    blocks.append(
+                        jnp.concatenate(
+                            [sums[i * width : (i + 1) * width], found[3], norm], axis=0
+                        )
+                    )
+                sub = lax.rem(j, steps) * here + part * group + i
+                at_row = (sub * parts + lax.div(j, steps)) * held
+                keep_ref[pl.ds(at_row, held), :] = jnp.where(first_core, blocks[0], blocks[1])
+                give_ref[pl.ds(at_row, held), :] = jnp.where(first_core, blocks[1], blocks[0])
         return 0
 
-    lax.fori_loop(0, dims // COLS, columns, 0)
+    for j in range(dims // COLS):
+        columns(j, 0)
     nc_copy.wait()
 
 
@@ -244,25 +301,24 @@
     rows = arrived.shape[0]
     lists, dims = centroids.shape
     tiles = dims // LANES
-    here = COLS // width
+    group = LANES // width
     sums = jax.ShapeDtypeStruct((subs * (width + 2), LANES), jnp.float32)
     return pl.pallas_call(
         functools.partial(local_kernel, subs, width, parts, prior, 256),
-        in_specs=[
-            pl.BlockSpec(memory_space=pltpu.SMEM),
-            IN_VMEM,
-            IN_VMEM,
-        ],
+        in_specs=[pl.BlockSpec(memory_space=pltpu.SMEM), IN_VMEM, IN_VMEM],
         out_specs=[pl.BlockSpec(memory_space=pl.ANY), IN_VMEM, IN_VMEM],
         out_shape=[jax.ShapeDtypeStruct((lists, dims), jnp.float32), sums, sums],
         scratch_shapes=[
             pltpu.VMEM((lists, rows), jnp.bfloat16),
             pltpu.VMEM((lists, LANES), jnp.float32),
-            pltpu.VMEM((subs // here, here, rows), jnp.int32),
+            pltpu.VMEM((subs // group, group, rows), jnp.int32),
             pltpu.VMEM((lists * tiles, LANES), jnp.float32),
             pltpu.VMEM((rows * tiles, LANES), jnp.float32),
+            pltpu.VMEM((rows, dims), jnp.bfloat16),
+            pltpu.VMEM((rows, dims), jnp.bfloat16),
+            pltpu.VMEM((rows, LANES), jnp.float32),
+            pltpu.VMEM((rows, 4 * LANES), jnp.bfloat16),
             pltpu.VMEM((rows, COLS), jnp.bfloat16),
-            pltpu.VMEM((rows, LANES), jnp.bfloat16),
             pltpu.VMEM((1, rows), jnp.int32),
             pltpu.SMEM((1, rows), jnp.int32),
             pltpu.VMEM((lists, dims), jnp.float32),

time: 101 us -> 98.3 us (0.973)
  Pallas kernels: 18.5 us -> 15.8 us
    pallas_call x1, Pallas kernels: 14.8 us -> 12 us  [local_pass(): pl.pallas_call(functools.partial(local_kernel, subs, width, parts, prior,...]
where the time goes in v5:
time: 98.3 us; the launch traced here: 98 us
  blocking collectives  55 us (56%)
  Pallas kernels  15.8 us (16%)
  waiting for transfers between devices  15.7 us (16%)
  starting transfers between devices  9.9 us (10%)
    all_to_all x1, blocking collectives, on_device(): lax.all_to_all(sent, SPLIT, split_axis=0, concat_axis=0, tiled=True)  43.8 us
    all_to_all x1, waiting for transfers between devices, on_device(): lax.all_to_all(paired.reshape(chips * parts, 1, held * LANES), ('chip', '...  12.9 us
    pallas_call x1, Pallas kernels, local_pass(): pl.pallas_call(functools.partial(local_kernel, subs, width, parts, prior,...  12 us
    all_to_all x1, blocking collectives, on_device(): lax.all_to_all(done.reshape(chips, 1, held * LANES), 'chip', split_axis=0...  11.2 us
    all_to_all x1, starting transfers between devices, on_device(): lax.all_to_all(paired.reshape(chips * parts, 1, held * LANES), ('chip', '...  4.85 us
    ppermute x1, starting transfers between devices, on_device(): other = lax.ppermute(half, 'core', swap)  3.43 us
    pallas_call x1, Pallas kernels, pack(): pl.pallas_call(functools.partial(pack_kernel, lists, pieces), in_specs=[a...  2.71 us
  transfers between devices with their start and end apart: 3, of which 3 were waited for; matrix products, arithmetic and copies ran while one was open for 0% of the time, Pallas kernels for 0%

profile of v5, /device:TPU:1, one launch (start us, length us, event | category | flops | bytes accessed | tf_op | source)
XLA Modules:
  0.0 98.0 jit_solution(7374612870188333556)
XLA Ops:
  0.6 0.0 copy-start
  0.7 2.7 %pack.1 = bf16[1024,1152]{1,0:T(8,128)(2,1)} custom-call(bf16[1024,1024]{1,0:T(8,128)(2,1)} %v_ref.1, s32[1,1024]{1,0:T(1,128)} %bitcast.18, s32[64,1024]{1,0:T(8,128)} %bitcast.17), custom_call_target="tpu_custom_call" | custom-call | tf_op jit(solution)/shard_map/pack/pallas_call | solution.py:80
  3.4 0.0 copy-start.1
  3.4 43.8 %all_to_all.21 = bf16[128,8,1152]{2,1,0:T(8,128)(2,1)S(1)} all-to-all(bf16[128,8,1152]{2,1,0:T(8,128)(2,1)} %bitcast.16), channel_id=1, replica_groups=mesh['chip'=32,'core'=2,'sub'=2] {'chip','core','sub'}, dimensions={0} | all-to-all | bytes 4718592 | tf_op jit(solution)/shard_map/all_to_all | solution.py:386
  47.2 0.0 copy-done.1
  47.2 12.0 %local_pass.1 = (f32[512,1024]{1,0:T(8,128)}, f32[1152,128]{1,0:T(8,128)S(1)}, f32[1152,128]{1,0:T(8,128)S(1)}) custom-call(s32[1]{0:T(128)} %bitcast.2.core_ref, bf16[1024,1152]{1,0:T(8,128)(2,1)S(1)} %bitcast.11, bf16[512,1024]{1,0:T(8,128)(2,1)S(1)} %copy-done.1), custom_call_target="tpu_custom_call" | custom-call | tf_op jit(solution)/shard_map/local_pass/pallas_call | solution.py:306
  59.3 1.6 %collective-permute-start = (f32[1152,128]{1,0:T(8,128)S(1)}, f32[1152,128]{1,0:T(8,128)S(1)}, u32[]{:S(2)}, u32[]{:S(2)}) collective-permute-start(f32[1152,128]{1,0:T(8,128)S(1)} %get-tuple-element.14), channel_id=1, source_target_pairs={{0,2},{2,0},{1,3},{3,1},{4,6},{6,4},{5,7},{7,5},{8,10},{10,8},{9,1... | collective-permute-start | bytes 1769480 | tf_op jit(solution)/shard_map/ppermute | solution.py:390
  60.9 1.6 %collective-permute-done = f32[1152,128]{1,0:T(8,128)S(1)} collective-permute-done((f32[1152,128]{1,0:T(8,128)S(1)}, f32[1152,128]{1,0:T(8,128)S(1)}, u32[]{:S(2)}, u32[]{:S(2)}) %collective-permute-start) | collective-permute-done | bytes 589856 | tf_op jit(solution)/shard_map/ppermute | solution.py:390
  62.5 0.9 add.9
  63.4 4.8 %all-to-all-start.1 = ((f32[64,1,2304]{2,1,0:T(1,128)}), f32[64,1,2304]{2,1,0:T(1,128)S(1)}, u32[]{:S(2)}, u32[]{:S(2)}) async-start(f32[64,1,2304]{2,1,0:T(1,128)} %bitcast.5), calls=%async_computation.1 | async-start | bytes 1179648 | tf_op jit(solution)/shard_map/all_to_all | solution.py:392
  68.3 0.0 copy-done
  68.3 12.9 %all-to-all-done.1 = f32[64,1,2304]{2,1,0:T(1,128)S(1)} async-done(((f32[64,1,2304]{2,1,0:T(1,128)}), f32[64,1,2304]{2,1,0:T(1,128)S(1)}, u32[]{:S(2)}, u32[]{:S(2)}) %all-to-all-start.1) | async-done | bytes 589856 | tf_op jit(solution)/shard_map/all_to_all | solution.py:392
  81.2 0.2 owner_pass.1
  81.4 11.2 %all_to_all.22 = f32[32,1,2176]{2,1,0:T(1,128)S(1)} all-to-all(f32[32,1,2176]{2,1,0:T(1,128)S(1)} %bitcast.15), channel_id=1, replica_groups=mesh['chip'=32,'core'=2,'sub'=2] {'chip'}, dimensions={0} | all-to-all | bytes 557056 | tf_op jit(solution)/shard_map/all_to_all | solution.py:411
  92.5 3.4 %collective-permute-start.1 = (f32[544,128]{1,0:T(8,128)S(1)}, f32[544,128]{1,0:T(8,128)S(1)}, u32[]{:S(2)}, u32[]{:S(2)}) collective-permute-start(f32[544,128]{1,0:T(8,128)S(1)} %bitcast.13), channel_id=1, source_target_pairs={{0,2},{2,0},{1,3},{3,1},{4,6},{6,4},{5,7},{7,5},{8,10},{10,8},{9,1... | collective-permute-start | bytes 835592 | tf_op jit(solution)/shard_map/ppermute | solution.py:414
  96.0 1.2 %collective-permute-done.1.other_ref = f32[544,128]{1,0:T(8,128)S(1)} collective-permute-done((f32[544,128]{1,0:T(8,128)S(1)}, f32[544,128]{1,0:T(8,128)S(1)}, u32[]{:S(2)}, u32[]{:S(2)}) %collective-permute-start.1) | collective-permute-done | bytes 278560 | tf_op jit(solution)/shard_map/ppermute | solution.py:414
  97.2 0.8 finish.1
  (1 shorter events, 0.0 us)
Async XLA Ops:
  0.6 67.6 %copy-start = (f32[32,16,256]{2,1,0:T(8,128)S(1)}, f32[32,16,256]{2,1,0:T(8,128)}, u32[]{:S(2)}) copy-start(f32[32,16,256]{2,1,0:T(8,128)} %param.9) | copy-start | bytes 1572868
  3.4 43.9 %copy-start.1 = (bf16[512,1024]{1,0:T(8,128)(2,1)S(1)}, bf16[512,1024]{1,0:T(8,128)(2,1)}, u32[]{:S(2)}) copy-start(bf16[512,1024]{1,0:T(8,128)(2,1)} %cent_ref.1) | copy-start | bytes 3145732
  59.3 3.3 %collective-permute-start = (f32[1152,128]{1,0:T(8,128)S(1)}, f32[1152,128]{1,0:T(8,128)S(1)}, u32[]{:S(2)}, u32[]{:S(2)}) collective-permute-start(f32[1152,128]{1,0:T(8,128)S(1)} %get-tuple-element.14), channel_id=1, source_target_pairs={{0,2},{2,0},{1,3},{3,1},{4,6},{6,4},{5,7},{7,5},{8,10},{10,8},{9,1... | collective-permute-start | bytes 1769480 | tf_op jit(solution)/shard_map/ppermute | solution.py:390
  63.4 17.8 %all-to-all-start.1 = ((f32[64,1,2304]{2,1,0:T(1,128)}), f32[64,1,2304]{2,1,0:T(1,128)S(1)}, u32[]{:S(2)}, u32[]{:S(2)}) async-start(f32[64,1,2304]{2,1,0:T(1,128)} %bitcast.5), calls=%async_computation.1 | async-start | bytes 1179648 | tf_op jit(solution)/shard_map/all_to_all | solution.py:392
  92.5 4.6 %collective-permute-start.1 = (f32[544,128]{1,0:T(8,128)S(1)}, f32[544,128]{1,0:T(8,128)S(1)}, u32[]{:S(2)}, u32[]{:S(2)}) collective-permute-start(f32[544,128]{1,0:T(8,128)S(1)} %bitcast.13), channel_id=1, source_target_pairs={{0,2},{2,0},{1,3},{3,1},{4,6},{6,4},{5,7},{7,5},{8,10},{10,8},{9,1... | collective-permute-start | bytes 835592 | tf_op jit(solution)/shard_map/ppermute | solution.py:414

commit v6 on v5

--- a/solution.py
+++ b/solution.py
@@ -28,26 +28,30 @@
 
 
 def pack_kernel(
-    lists, pieces, v_ref, ids_ref, codes_ref, out_ref, held, ids_v, codes_v, ins, outs
+    lists, pieces, place, v_ref, ids_ref, codes_ref, books_ref, out_ref, old_ref, ids_v, codes_v, sems
 ):
     rows, dims = v_ref.shape
     subs = codes_ref.shape[0]
     step = rows // pieces
-    first = [
-        pltpu.make_async_copy(codes_ref, codes_v, ins.at[pieces]),
-        pltpu.make_async_copy(ids_ref, ids_v, ins.at[pieces + 1]),
+    half = pl.ds(pl.multiple_of(place[1] * LANES, LANES), LANES)
+    small = [
+        pltpu.make_async_copy(codes_ref, codes_v, sems.at[pieces]),
+        pltpu.make_async_copy(ids_ref, ids_v, sems.at[pieces + 1]),
     ]
     moves = [
         pltpu.make_async_copy(
             v_ref.at[pl.ds(i * step, step)],
-            held.at[pl.ds(i * step, step), pl.ds(0, dims)],
-            ins.at[i],
+            out_ref.at[pl.ds(i * step, step), pl.ds(0, dims)],
+            sems.at[i],
         )
         for i in range(pieces)
     ]
-    for move in first + moves:
+    moves.append(
+        pltpu.make_async_copy(books_ref.at[place[0], :, half], old_ref, sems.at[pieces + 2])
+    )
+    for move in small + moves:
         move.start()
-    for move in first:
+    for move in small:
         move.wait()
     ids = lax.rem(ids_v[...], lists)
     high = lax.div(ids, 256)
@@ -60,38 +64,34 @@
         ],
         axis=0,
     )
-    held[:, dims:] = jnp.transpose(aux).astype(jnp.bfloat16)
-    sends = []
-    for i, move in enumerate(moves):
+    out_ref[:, dims:] = jnp.transpose(aux).astype(jnp.bfloat16)
+    for move in moves:
         move.wait()
-        at = pl.ds(i * step, step)
-        send = pltpu.make_async_copy(held.at[at], out_ref.at[at], outs.at[i])
-        send.start()
-        sends.append(send)
-    for send in sends:
-        send.wait()
-
-
-def pack(vectors, list_ids, codes, lists):
+
+
+def pack(place, vectors, list_ids, codes, codebooks, lists):
     rows, dims = vectors.shape
     subs = codes.shape[1]
-    pieces = 8
+    width = codebooks.shape[1]
+    pieces = 4
     anywhere = pl.BlockSpec(memory_space=pl.ANY)
+    sources = (vectors, list_ids.reshape(1, rows), jnp.transpose(codes), codebooks)
     return pl.pallas_call(
         functools.partial(pack_kernel, lists, pieces),
-        in_specs=[anywhere] * 3,
-        out_specs=anywhere,
-        out_shape=jax.ShapeDtypeStruct((rows, dims + LANES), jnp.bfloat16),
+        in_specs=[pl.BlockSpec(memory_space=pltpu.SMEM)] + [anywhere] * 4,
+        out_specs=[IN_VMEM, IN_VMEM],
+        out_shape=[
+            jax.ShapeDtypeStruct((rows, dims + LANES), jnp.bfloat16),
+            jax.ShapeDtypeStruct((width, LANES), jnp.float32),
+        ],
         scratch_shapes=[
-            pltpu.VMEM((rows, dims + LANES), jnp.bfloat16),
             pltpu.VMEM((1, rows), jnp.int32),
             pltpu.VMEM((subs, rows), jnp.int32),
-            pltpu.SemaphoreType.DMA((pieces + 2,)),
-            pltpu.SemaphoreType.DMA((pieces,)),
+            pltpu.SemaphoreType.DMA((pieces + 3,)),
         ],
-        compiler_params=pltpu.CompilerParams(vmem_limit_bytes=58 * MIB),
+        compiler_params=pltpu.CompilerParams(vmem_limit_bytes=12 * MIB),
         name="pack",
-    )(vectors, list_ids.reshape(1, rows), jnp.transpose(codes))
+    )(place, *[pltpu.with_memory_space_constraint(x, pltpu.HBM) for x in sources])
 
 
 def local_kernel(
@@ -382,7 +382,8 @@
     core_arg = core.astype(jnp.int32).reshape(1)
     swap = [(0, 1), (1, 0)]
 
-    sent, core_arg = lax.optimization_barrier((pack(vectors, list_ids, codes, lists), core_arg))
+    place = jnp.stack([lax.axis_index("chip"), core]).astype(jnp.int32)
+    sent, old = pack(place, vectors, list_ids, codes, codebooks, lists)
     arrived = lax.all_to_all(sent, SPLIT, split_axis=0, concat_axis=0, tiled=True)
     new_centroids, keep, give = local_pass(
         core_arg, arrived, centroids, subs, width, prior_lists, parts
@@ -396,9 +397,6 @@
         concat_axis=0,
         tiled=True,
     ).reshape(chips * parts * held, LANES)
-    old = lax.dynamic_slice(
-        codebooks, (lax.axis_index("chip"), 0, core * LANES), (1, width, LANES)
-    )[0]
     held = width + 1
     done = pl.pallas_call(
         functools.partial(owner_kernel, width, prior_codes, chips),

time: 98.3 us -> 96.6 us (0.983)
  blocking collectives: 55 us -> 72.4 us
  waiting for transfers between devices: 15.7 us -> 2.82 us
  starting transfers between devices: 9.9 us -> 5.04 us
    all_to_all x0 -> x1, blocking collectives: none -> 17.6 us  [on_device(): lax.all_to_all(paired.reshape(chips * parts, 1, held * LANES), ('chip', '...]
    all_to_all x1 -> x0, waiting for transfers between devices: 12.9 us -> none  [on_device(): lax.all_to_all(paired.reshape(chips * parts, 1, held * LANES), ('chip', '...]
    all_to_all x1 -> x0, starting transfers between devices: 4.85 us -> none  [on_device(): lax.all_to_all(paired.reshape(chips * parts, 1, held * LANES), ('chip', '...]
  transfers between devices with their start and end apart: 3 -> 2, of which waited for: 3 -> 2; matrix products, arithmetic and copies ran while one was open for 0% -> 0% of each run, Pallas kernels for 0% -> 0%
where the time goes in v6:
time: 96.6 us; the launch traced here: 96.3 us
  blocking collectives  72.4 us (75%)
  Pallas kernels  15.3 us (16%)
  starting transfers between devices  5.04 us (5%)
  waiting for transfers between devices  2.82 us (3%)
    all_to_all x1, blocking collectives, on_device(): lax.all_to_all(sent, SPLIT, split_axis=0, concat_axis=0, tiled=True)  43.6 us
    all_to_all x1, blocking collectives, on_device(): lax.all_to_all(paired.reshape(chips * parts, 1, held * LANES), ('chip', '...  17.6 us
    pallas_call x1, Pallas kernels, local_pass(): pl.pallas_call(functools.partial(local_kernel, subs, width, parts, prior,...  12 us
    all_to_all x1, blocking collectives, on_device(): lax.all_to_all(done.reshape(chips, 1, held * LANES), 'chip', split_axis=0...  11.2 us
    ppermute x1, starting transfers between devices, on_device(): other = lax.ppermute(half, 'core', swap)  3.43 us
    pallas_call x1, Pallas kernels, pack(): pl.pallas_call(functools.partial(pack_kernel, lists, pieces), in_specs=[p...  2.22 us
  transfers between devices with their start and end apart: 2, of which 2 were waited for; matrix products, arithmetic and copies ran while one was open for 0% of the time, Pallas kernels for 0%

profile of v6, /device:TPU:1, one launch (start us, length us, event | category | flops | bytes accessed | tf_op | source)
XLA Modules:
  0.0 96.3 jit_solution(9825112541805667500)
XLA Ops:
  0.6 0.1 pad_add_fusion.place
  0.7 2.2 %pack.1 = (bf16[1024,1152]{1,0:T(8,128)(2,1)S(1)}, f32[16,128]{1,0:T(8,128)S(1)}) custom-call(s32[2]{0:T(128)S(1)} %pad_add_fusion.place, bf16[1024,1024]{1,0:T(8,128)(2,1)} %v_ref.1, s32[1,1024]{1,0:T(1,128)} %bitcast.18, s32[64,1024]{1,0:T(8,128)} %bitcast.17, f32[32,16,256]{2,1,0:T(8,128)} %books_ref.1), custom_call_target="tpu_custom_call" | custom-call | tf_op jit(solution)/shard_map/pack/pallas_call | solution.py:79
  2.9 0.0 copy-start
  2.9 43.6 %all_to_all.21 = bf16[128,8,1152]{2,1,0:T(8,128)(2,1)S(1)} all-to-all(bf16[128,8,1152]{2,1,0:T(8,128)(2,1)S(1)} %bitcast.11), channel_id=1, replica_groups=mesh['chip'=32,'core'=2,'sub'=2] {'chip','core','sub'}, dimensions={0} | all-to-all | bytes 4718592 | tf_op jit(solution)/shard_map/all_to_all | solution.py:387
  46.6 0.0 copy-done
  46.6 12.0 %local_pass.1 = (f32[512,1024]{1,0:T(8,128)}, f32[1152,128]{1,0:T(8,128)S(1)}, f32[1152,128]{1,0:T(8,128)S(1)}) custom-call(s32[1]{0:T(128)} %bitcast.core_ref, bf16[1024,1152]{1,0:T(8,128)(2,1)S(1)} %bitcast.10, bf16[512,1024]{1,0:T(8,128)(2,1)S(1)} %copy-done), custom_call_target="tpu_custom_call" | custom-call | tf_op jit(solution)/shard_map/local_pass/pallas_call | solution.py:306
  58.6 1.6 %collective-permute-start = (f32[1152,128]{1,0:T(8,128)S(1)}, f32[1152,128]{1,0:T(8,128)S(1)}, u32[]{:S(2)}, u32[]{:S(2)}) collective-permute-start(f32[1152,128]{1,0:T(8,128)S(1)} %get-tuple-element.13), channel_id=1, source_target_pairs={{0,2},{2,0},{1,3},{3,1},{4,6},{6,4},{5,7},{7,5},{8,10},{10,8},{9,1... | collective-permute-start | bytes 1769480 | tf_op jit(solution)/shard_map/ppermute | solution.py:391
  60.2 1.6 %collective-permute-done = f32[1152,128]{1,0:T(8,128)S(1)} collective-permute-done((f32[1152,128]{1,0:T(8,128)S(1)}, f32[1152,128]{1,0:T(8,128)S(1)}, u32[]{:S(2)}, u32[]{:S(2)}) %collective-permute-start) | collective-permute-done | bytes 589856 | tf_op jit(solution)/shard_map/ppermute | solution.py:391
  61.9 0.1 add.3
  61.9 17.6 %all_to_all.22 = f32[64,1,2304]{2,1,0:T(1,128)S(1)} all-to-all(f32[64,1,2304]{2,1,0:T(1,128)S(1)} %bitcast.16), channel_id=1, replica_groups=mesh['chip'=32,'core'=2,'sub'=2] {'chip','sub'}, dimensions={0} | all-to-all | bytes 1179648 | tf_op jit(solution)/shard_map/all_to_all | solution.py:393
  79.5 0.2 owner_pass.1
  79.7 11.2 %all_to_all.23 = f32[32,1,2176]{2,1,0:T(1,128)S(1)} all-to-all(f32[32,1,2176]{2,1,0:T(1,128)S(1)} %bitcast.15), channel_id=1, replica_groups=mesh['chip'=32,'core'=2,'sub'=2] {'chip'}, dimensions={0} | all-to-all | bytes 557056 | tf_op jit(solution)/shard_map/all_to_all | solution.py:409
  90.9 3.4 %collective-permute-start.1 = (f32[544,128]{1,0:T(8,128)S(1)}, f32[544,128]{1,0:T(8,128)S(1)}, u32[]{:S(2)}, u32[]{:S(2)}) collective-permute-start(f32[544,128]{1,0:T(8,128)S(1)} %bitcast.13), channel_id=1, source_target_pairs={{0,2},{2,0},{1,3},{3,1},{4,6},{6,4},{5,7},{7,5},{8,10},{10,8},{9,1... | collective-permute-start | bytes 835592 | tf_op jit(solution)/shard_map/ppermute | solution.py:412
  94.3 1.2 %collective-permute-done.1.other_ref = f32[544,128]{1,0:T(8,128)S(1)} collective-permute-done((f32[544,128]{1,0:T(8,128)S(1)}, f32[544,128]{1,0:T(8,128)S(1)}, u32[]{:S(2)}, u32[]{:S(2)}) %collective-permute-start.1) | collective-permute-done | bytes 278560 | tf_op jit(solution)/shard_map/ppermute | solution.py:412
  95.5 0.8 finish.1
Async XLA Ops:
  2.9 43.7 %copy-start = (bf16[512,1024]{1,0:T(8,128)(2,1)S(1)}, bf16[512,1024]{1,0:T(8,128)(2,1)}, u32[]{:S(2)}) copy-start(bf16[512,1024]{1,0:T(8,128)(2,1)} %cent_ref.1) | copy-start | bytes 3145732
  58.6 3.2 %collective-permute-start = (f32[1152,128]{1,0:T(8,128)S(1)}, f32[1152,128]{1,0:T(8,128)S(1)}, u32[]{:S(2)}, u32[]{:S(2)}) collective-permute-start(f32[1152,128]{1,0:T(8,128)S(1)} %get-tuple-element.13), channel_id=1, source_target_pairs={{0,2},{2,0},{1,3},{3,1},{4,6},{6,4},{5,7},{7,5},{8,10},{10,8},{9,1... | collective-permute-start | bytes 1769480 | tf_op jit(solution)/shard_map/ppermute | solution.py:391
  90.9 4.6 %collective-permute-start.1 = (f32[544,128]{1,0:T(8,128)S(1)}, f32[544,128]{1,0:T(8,128)S(1)}, u32[]{:S(2)}, u32[]{:S(2)}) collective-permute-start(f32[544,128]{1,0:T(8,128)S(1)} %bitcast.13), channel_id=1, source_target_pairs={{0,2},{2,0},{1,3},{3,1},{4,6},{6,4},{5,7},{7,5},{8,10},{10,8},{9,1... | collective-permute-start | bytes 835592 | tf_op jit(solution)/shard_map/ppermute | solution.py:412

commit v7 on v6

--- a/solution.py
+++ b/solution.py
@@ -154,15 +154,13 @@
     inside = jnp.where((both < LANES) == (lane < subs), 1.0, 0.0)
     side_v[:, 3 * LANES :] = inside.astype(jnp.bfloat16)
 
-    for j in range(dims // COLS):
-        totals = dot(hot[...], arr_ref[:, j * COLS : (j + 1) * COLS])
-        for h in range(side):
-            tile = j * side + h
-            at = slice(tile * LANES, (tile + 1) * LANES)
-            old = prior * cent_ref[:, at].astype(jnp.float32)
-            nc = (totals[:, h * LANES : (h + 1) * LANES] + old) * inv[...]
-            nc_v[:, at] = nc
-            table[pl.ds(tile, lists, stride=tiles), :] = nc
+    totals = dot(hot[...], arr_ref[:, :dims])
+    for tile in range(tiles):
+        at = slice(tile * LANES, (tile + 1) * LANES)
+        old = prior * cent_ref[:, at].astype(jnp.float32)
+        nc = (totals[:, at] + old) * inv[...]
+        nc_v[:, at] = nc
+        table[pl.ds(tile, lists, stride=tiles), :] = nc
     nc_copy = pltpu.make_async_copy(nc_v, nc_ref, nc_sem)
     nc_copy.start()
     copy.wait()
@@ -174,7 +172,7 @@
             picked[pl.ds(pl.multiple_of(r * tiles, 8), tiles), :] = row
         return 0
 
-    lax.fori_loop(0, rows // 8, pick, 0)
+    lax.fori_loop(0, rows // 8, pick, 0, unroll=8)
 
     def residuals(j, _):
         at = pl.ds(pl.multiple_of(j * COLS, COLS), COLS)
@@ -207,7 +205,7 @@
             norms[ra, :] = jnp.where(j == 0, found, norms[ra, :] + found)
         return 0
 
-    lax.fori_loop(0, dims // COLS, residuals, 0)
+    lax.fori_loop(0, dims // COLS, residuals, 0, unroll=2)
 
     for i in range(rows // chunk):
         ra = slice(i * chunk, (i + 1) * chunk)
@@ -230,19 +228,20 @@
         )
         wanted = kind * LANES + half * subs + sub
         move = jnp.where((line == wanted) & (kind < kinds), 1.0, 0.0).astype(jnp.bfloat16)
-        for i in range(rows // chunk):
-            ra = slice(i * chunk, (i + 1) * chunk)
+        for i in range(2 * rows // chunk):
+            ra = slice(i * chunk // 2, (i + 1) * chunk // 2)
             extra[ra, :] = dot(side_v[ra, :], move).astype(jnp.bfloat16)
 
         level = lax.broadcasted_iota(jnp.int32, (LANES, rows), 0)
+        level = level.astype(jnp.float32).astype(jnp.bfloat16)
+        one = jnp.ones((), jnp.bfloat16)
+        zero = jnp.zeros((), jnp.bfloat16)
         lane = lax.broadcasted_iota(jnp.int32, (LANES, LANES), 1)
         wide_lane = lax.broadcasted_iota(jnp.int32, (rows, LANES), 1)
         steps = subs // parts // here
         for part in range(side):
             at = pl.ds(pl.multiple_of(j * COLS + part * LANES, LANES), LANES)
-            codes = code_t[j * side + part]
-            codes16 = codes.astype(jnp.float32).astype(jnp.bfloat16)
-            level16 = level.astype(jnp.float32).astype(jnp.bfloat16)
+            codes = code_t[j * side + part].astype(jnp.float32).astype(jnp.bfloat16)
             beside = extra[:, part * LANES : (part + 1) * LANES]
             low_sum = jnp.zeros((LANES, LANES), jnp.float32)
             high_sum = low_sum
@@ -254,7 +253,7 @@
                 apart = (lane >= LANES // 2) == (q == 0)
                 onehot = jnp.concatenate(
                     [
-                        jnp.where(level16 == codes16[i : i + 1], jnp.ones((), jnp.bfloat16), jnp.zeros((), jnp.bfloat16))
+                        jnp.where(level == codes[i : i + 1], one, zero)
                         for i in range(q * quad, (q + 1) * quad)
                     ],
                     axis=0,

time: 96.6 us -> 95.7 us (level)
  Pallas kernels: 15.3 us -> 14.3 us
where the time goes in v7:
time: 95.7 us; the launch traced here: 95.4 us
  blocking collectives  72.4 us (76%)
  Pallas kernels  14.3 us (15%)
  starting transfers between devices  5.05 us (5%)
  waiting for transfers between devices  2.82 us (3%)
    all_to_all x1, blocking collectives, on_device(): lax.all_to_all(sent, SPLIT, split_axis=0, concat_axis=0, tiled=True)  43.6 us
    all_to_all x1, blocking collectives, on_device(): lax.all_to_all(paired.reshape(chips * parts, 1, held * LANES), ('chip', '...  17.6 us
    all_to_all x1, blocking collectives, on_device(): lax.all_to_all(done.reshape(chips, 1, held * LANES), 'chip', split_axis=0...  11.2 us
    pallas_call x1, Pallas kernels, local_pass(): pl.pallas_call(functools.partial(local_kernel, subs, width, parts, prior,...  11.1 us
    ppermute x1, starting transfers between devices, on_device(): other = lax.ppermute(half, 'core', swap)  3.43 us
    pallas_call x1, Pallas kernels, pack(): pl.pallas_call(functools.partial(pack_kernel, lists, pieces), in_specs=[p...  2.22 us
  transfers between devices with their start and end apart: 2, of which 2 were waited for; matrix products, arithmetic and copies ran while one was open for 0% of the time, Pallas kernels for 0%

profile of v7, /device:TPU:1, one launch (start us, length us, event | category | flops | bytes accessed | tf_op | source)
XLA Modules:
  0.0 95.4 jit_solution(13144839028922704976)
XLA Ops:
  0.6 0.1 pad_add_fusion.place
  0.7 2.2 %pack.1 = (bf16[1024,1152]{1,0:T(8,128)(2,1)S(1)}, f32[16,128]{1,0:T(8,128)S(1)}) custom-call(s32[2]{0:T(128)S(1)} %pad_add_fusion.place, bf16[1024,1024]{1,0:T(8,128)(2,1)} %v_ref.1, s32[1,1024]{1,0:T(1,128)} %bitcast.18, s32[64,1024]{1,0:T(8,128)} %bitcast.17, f32[32,16,256]{2,1,0:T(8,128)} %books_ref.1), custom_call_target="tpu_custom_call" | custom-call | tf_op jit(solution)/shard_map/pack/pallas_call | solution.py:79
  2.9 0.0 copy-start
  2.9 43.6 %all_to_all.21 = bf16[128,8,1152]{2,1,0:T(8,128)(2,1)S(1)} all-to-all(bf16[128,8,1152]{2,1,0:T(8,128)(2,1)S(1)} %bitcast.11), channel_id=1, replica_groups=mesh['chip'=32,'core'=2,'sub'=2] {'chip','core','sub'}, dimensions={0} | all-to-all | bytes 4718592 | tf_op jit(solution)/shard_map/all_to_all | solution.py:386
  46.6 0.0 copy-done
  46.6 11.1 %local_pass.1 = (f32[512,1024]{1,0:T(8,128)}, f32[1152,128]{1,0:T(8,128)S(1)}, f32[1152,128]{1,0:T(8,128)S(1)}) custom-call(s32[1]{0:T(128)} %bitcast.core_ref, bf16[1024,1152]{1,0:T(8,128)(2,1)S(1)} %bitcast.10, bf16[512,1024]{1,0:T(8,128)(2,1)S(1)} %copy-done), custom_call_target="tpu_custom_call" | custom-call | tf_op jit(solution)/shard_map/local_pass/pallas_call | solution.py:305
  57.7 1.6 %collective-permute-start = (f32[1152,128]{1,0:T(8,128)S(1)}, f32[1152,128]{1,0:T(8,128)S(1)}, u32[]{:S(2)}, u32[]{:S(2)}) collective-permute-start(f32[1152,128]{1,0:T(8,128)S(1)} %get-tuple-element.13), channel_id=1, source_target_pairs={{0,2},{2,0},{1,3},{3,1},{4,6},{6,4},{5,7},{7,5},{8,10},{10,8},{9,1... | collective-permute-start | bytes 1769480 | tf_op jit(solution)/shard_map/ppermute | solution.py:390
  59.3 1.6 %collective-permute-done = f32[1152,128]{1,0:T(8,128)S(1)} collective-permute-done((f32[1152,128]{1,0:T(8,128)S(1)}, f32[1152,128]{1,0:T(8,128)S(1)}, u32[]{:S(2)}, u32[]{:S(2)}) %collective-permute-start) | collective-permute-done | bytes 589856 | tf_op jit(solution)/shard_map/ppermute | solution.py:390
  60.9 0.1 add.3
  61.0 17.6 %all_to_all.22 = f32[64,1,2304]{2,1,0:T(1,128)S(1)} all-to-all(f32[64,1,2304]{2,1,0:T(1,128)S(1)} %bitcast.16), channel_id=1, replica_groups=mesh['chip'=32,'core'=2,'sub'=2] {'chip','sub'}, dimensions={0} | all-to-all | bytes 1179648 | tf_op jit(solution)/shard_map/all_to_all | solution.py:392
  78.6 0.2 owner_pass.1
  78.8 11.2 %all_to_all.23 = f32[32,1,2176]{2,1,0:T(1,128)S(1)} all-to-all(f32[32,1,2176]{2,1,0:T(1,128)S(1)} %bitcast.15), channel_id=1, replica_groups=mesh['chip'=32,'core'=2,'sub'=2] {'chip'}, dimensions={0} | all-to-all | bytes 557056 | tf_op jit(solution)/shard_map/all_to_all | solution.py:408
  90.0 3.4 %collective-permute-start.1 = (f32[544,128]{1,0:T(8,128)S(1)}, f32[544,128]{1,0:T(8,128)S(1)}, u32[]{:S(2)}, u32[]{:S(2)}) collective-permute-start(f32[544,128]{1,0:T(8,128)S(1)} %bitcast.13), channel_id=1, source_target_pairs={{0,2},{2,0},{1,3},{3,1},{4,6},{6,4},{5,7},{7,5},{8,10},{10,8},{9,1... | collective-permute-start | bytes 835592 | tf_op jit(solution)/shard_map/ppermute | solution.py:411
  93.4 1.2 %collective-permute-done.1.other_ref = f32[544,128]{1,0:T(8,128)S(1)} collective-permute-done((f32[544,128]{1,0:T(8,128)S(1)}, f32[544,128]{1,0:T(8,128)S(1)}, u32[]{:S(2)}, u32[]{:S(2)}) %collective-permute-start.1) | collective-permute-done | bytes 278560 | tf_op jit(solution)/shard_map/ppermute | solution.py:411
  94.6 0.8 finish.1
Async XLA Ops:
  2.9 43.7 %copy-start = (bf16[512,1024]{1,0:T(8,128)(2,1)S(1)}, bf16[512,1024]{1,0:T(8,128)(2,1)}, u32[]{:S(2)}) copy-start(bf16[512,1024]{1,0:T(8,128)(2,1)} %cent_ref.1) | copy-start | bytes 3145732
  57.7 3.2 %collective-permute-start = (f32[1152,128]{1,0:T(8,128)S(1)}, f32[1152,128]{1,0:T(8,128)S(1)}, u32[]{:S(2)}, u32[]{:S(2)}) collective-permute-start(f32[1152,128]{1,0:T(8,128)S(1)} %get-tuple-element.13), channel_id=1, source_target_pairs={{0,2},{2,0},{1,3},{3,1},{4,6},{6,4},{5,7},{7,5},{8,10},{10,8},{9,1... | collective-permute-start | bytes 1769480 | tf_op jit(solution)/shard_map/ppermute | solution.py:390
  90.0 4.6 %collective-permute-start.1 = (f32[544,128]{1,0:T(8,128)S(1)}, f32[544,128]{1,0:T(8,128)S(1)}, u32[]{:S(2)}, u32[]{:S(2)}) collective-permute-start(f32[544,128]{1,0:T(8,128)S(1)} %bitcast.13), channel_id=1, source_target_pairs={{0,2},{2,0},{1,3},{3,1},{4,6},{6,4},{5,7},{7,5},{8,10},{10,8},{9,1... | collective-permute-start | bytes 835592 | tf_op jit(solution)/shard_map/ppermute | solution.py:411

commit v8 on v7

--- a/solution.py
+++ b/solution.py
@@ -12,7 +12,11 @@
 CORES = 2
 MIB = 1024 * 1024
 IN_VMEM = pl.BlockSpec(memory_space=pltpu.VMEM)
-SPLIT = ("chip", "core", "sub")
+FAR = 2
+SPLIT = ("far", "plane", "core", "sub")
+CHIP = ("far", "plane")
+ROW_ORDER = ("plane", "core", "far", "sub")
+SUM_ORDER = ("sub", "plane", "far")
 
 
 def split3(x):
@@ -30,24 +34,25 @@
 def pack_kernel(
     lists, pieces, place, v_ref, ids_ref, codes_ref, books_ref, out_ref, old_ref, ids_v, codes_v, sems
 ):
-    rows, dims = v_ref.shape
-    subs = codes_ref.shape[0]
-    step = rows // pieces
+    far, runs, run, dims = v_ref.shape
+    subs, rows = codes_ref.shape
+    step = runs // pieces
     half = pl.ds(pl.multiple_of(place[1] * LANES, LANES), LANES)
     small = [
-        pltpu.make_async_copy(codes_ref, codes_v, sems.at[pieces]),
-        pltpu.make_async_copy(ids_ref, ids_v, sems.at[pieces + 1]),
+        pltpu.make_async_copy(codes_ref, codes_v, sems.at[far * pieces]),
+        pltpu.make_async_copy(ids_ref, ids_v, sems.at[far * pieces + 1]),
     ]
     moves = [
         pltpu.make_async_copy(
-            v_ref.at[pl.ds(i * step, step)],
-            out_ref.at[pl.ds(i * step, step), pl.ds(0, dims)],
-            sems.at[i],
+            v_ref.at[f, pl.ds(i * step, step)],
+            out_ref.at[pl.ds(i * step, step), f, :, pl.ds(0, dims)],
+            sems.at[f * pieces + i],
         )
+        for f in range(far)
         for i in range(pieces)
     ]
     moves.append(
-        pltpu.make_async_copy(books_ref.at[place[0], :, half], old_ref, sems.at[pieces + 2])
+        pltpu.make_async_copy(books_ref.at[place[0], :, half], old_ref, sems.at[far * pieces + 2])
     )
     for move in small + moves:
         move.start()
@@ -64,34 +69,43 @@
         ],
         axis=0,
     )
-    out_ref[:, dims:] = jnp.transpose(aux).astype(jnp.bfloat16)
+    aux = jnp.transpose(aux).astype(jnp.bfloat16).reshape(far, runs, run, LANES)
+    for f in range(far):
+        out_ref[:, f, :, dims:] = aux[f]
     for move in moves:
         move.wait()
 
 
-def pack(place, vectors, list_ids, codes, codebooks, lists):
+def pack(place, vectors, list_ids, codes, codebooks, lists, run):
     rows, dims = vectors.shape
     subs = codes.shape[1]
     width = codebooks.shape[1]
-    pieces = 4
+    pieces = 2
+    runs = rows // (FAR * run)
     anywhere = pl.BlockSpec(memory_space=pl.ANY)
-    sources = (vectors, list_ids.reshape(1, rows), jnp.transpose(codes), codebooks)
-    return pl.pallas_call(
+    sources = (
+        vectors.reshape(FAR, runs, run, dims),
+        list_ids.reshape(1, rows),
+        jnp.transpose(codes),
+        codebooks,
+    )
+    sent, old = pl.pallas_call(
         functools.partial(pack_kernel, lists, pieces),
         in_specs=[pl.BlockSpec(memory_space=pltpu.SMEM)] + [anywhere] * 4,
         out_specs=[IN_VMEM, IN_VMEM],
         out_shape=[
-            jax.ShapeDtypeStruct((rows, dims + LANES), jnp.bfloat16),
+            jax.ShapeDtypeStruct((runs, FAR, run, dims + LANES), jnp.bfloat16),
             jax.ShapeDtypeStruct((width, LANES), jnp.float32),
         ],
         scratch_shapes=[
             pltpu.VMEM((1, rows), jnp.int32),
             pltpu.VMEM((subs, rows), jnp.int32),
-            pltpu.SemaphoreType.DMA((pieces + 3,)),
+            pltpu.SemaphoreType.DMA((FAR * pieces + 3,)),
         ],
         compiler_params=pltpu.CompilerParams(vmem_limit_bytes=12 * MIB),
         name="pack",
     )(place, *[pltpu.with_memory_space_constraint(x, pltpu.HBM) for x in sources])
+    return sent.reshape(rows, dims + LANES), old
 
 
 def local_kernel(
@@ -285,8 +299,9 @@
                             [sums[i * width : (i + 1) * width], found[3], norm], axis=0
                         )
                     )
-                sub = lax.rem(j, steps) * here + part * group + i
-                at_row = (sub * parts + lax.div(j, steps)) * held
+                sub = (j % steps) * here + part * group + i
+                near = subs // parts // FAR
+                at_row = ((j // steps * near + sub % near) * FAR + sub // near) * held
                 keep_ref[pl.ds(at_row, held), :] = jnp.where(first_core, blocks[0], blocks[1])
                 give_ref[pl.ds(at_row, held), :] = jnp.where(first_core, blocks[1], blocks[0])
         return 0
@@ -369,7 +384,7 @@
 
 def on_device(vectors, list_ids, codes, centroids, codebooks):
     rows, dims = vectors.shape
-    chips = lax.axis_size("chip")
+    chips = lax.axis_size("far") * lax.axis_size("plane")
     parts = lax.axis_size("sub")
     owners = chips * CORES * parts
     lists = centroids.shape[0]
@@ -381,9 +396,10 @@
     core_arg = core.astype(jnp.int32).reshape(1)
     swap = [(0, 1), (1, 0)]
 
-    place = jnp.stack([lax.axis_index("chip"), core]).astype(jnp.int32)
-    sent, old = pack(place, vectors, list_ids, codes, codebooks, lists)
-    arrived = lax.all_to_all(sent, SPLIT, split_axis=0, concat_axis=0, tiled=True)
+    place = jnp.stack([lax.axis_index(CHIP), core]).astype(jnp.int32)
+    run = rows // (chips * CORES)
+    sent, old = pack(place, vectors, list_ids, codes, codebooks, lists, run)
+    arrived = lax.all_to_all(sent, ROW_ORDER, split_axis=0, concat_axis=0, tiled=True)
     new_centroids, keep, give = local_pass(
         core_arg, arrived, centroids, subs, width, prior_lists, parts
     )
@@ -391,7 +407,7 @@
     held = width + 2
     mine = lax.all_to_all(
         paired.reshape(chips * parts, 1, held * LANES),
-        ("chip", "sub"),
+        SUM_ORDER,
         split_axis=0,
         concat_axis=0,
         tiled=True,
@@ -406,7 +422,7 @@
         name="owner_pass",
     )(mine, old)
     half = lax.all_to_all(
-        done.reshape(chips, 1, held * LANES), "chip", split_axis=0, concat_axis=0, tiled=True
+        done.reshape(chips, 1, held * LANES), CHIP, split_axis=0, concat_axis=0, tiled=True
     ).reshape(chips * held, LANES)
     other = lax.ppermute(half, "core", swap)
     table, distortion = pl.pallas_call(
@@ -425,7 +441,7 @@
 
 def solution(mesh):
     parts = mesh.shape["sub"]
-    cores = Mesh(mesh.devices.reshape(-1, CORES, parts), SPLIT)
+    cores = Mesh(mesh.devices.reshape(FAR, -1, CORES, parts), SPLIT)
     in_specs = (
         P(SPLIT, None),
         P(SPLIT),

time: 95.7 us -> 95 us (level)
  starting transfers between devices: 5.05 us -> 3.23 us
    ppermute x1, starting transfers between devices: 1.61 us -> 0.09 us  [on_device(): paired = keep + lax.ppermute(give, 'core', swap)]
where the time goes in v8:
time: 95 us; the launch traced here: 94.7 us
  blocking collectives  73.1 us (77%)
  Pallas kernels  14.3 us (15%)
  starting transfers between devices  3.23 us (3%)
  waiting for transfers between devices  3.18 us (3%)
    all_to_all x1, blocking collectives, on_device(): lax.all_to_all(sent, ROW_ORDER, split_axis=0, concat_axis=0, tiled=True)  44.1 us
    all_to_all x1, blocking collectives, on_device(): lax.all_to_all(paired.reshape(chips * parts, 1, held * LANES), SUM_ORDER,...  17.4 us
    all_to_all x1, blocking collectives, on_device(): lax.all_to_all(done.reshape(chips, 1, held * LANES), CHIP, split_axis=0,...  11.6 us
    pallas_call x1, Pallas kernels, local_pass(): pl.pallas_call(functools.partial(local_kernel, subs, width, parts, prior,...  11.1 us
    ppermute x1, starting transfers between devices, on_device(): other = lax.ppermute(half, 'core', swap)  3.15 us
    pallas_call x1, Pallas kernels, pack(): pl.pallas_call(functools.partial(pack_kernel, lists, pieces), in_specs=[p...  2.22 us
    ppermute x1, waiting for transfers between devices, on_device(): paired = keep + lax.ppermute(give, 'core', swap)  1.99 us
  transfers between devices with their start and end apart: 2, of which 2 were waited for; matrix products, arithmetic and copies ran while one was open for 0% of the time, Pallas kernels for 0%

profile of v8, /device:TPU:1, one launch (start us, length us, event | category | flops | bytes accessed | tf_op | source)
XLA Modules:
  0.0 94.7 jit_solution(11161196949114559069)
XLA Ops:
  0.6 0.1 pad_add_fusion.place
  0.7 2.2 %pack.1 = (bf16[32,2,16,1152]{3,2,1,0:T(8,128)(2,1)S(1)}, f32[16,128]{1,0:T(8,128)S(1)}) custom-call(s32[2]{0:T(128)S(1)} %pad_add_fusion.place, bf16[2,32,16,1024]{3,2,1,0:T(8,128)(2,1)} %bitcast.18, s32[1,1024]{1,0:T(1,128)} %bitcast.20, s32[64,1024]{1,0:T(8,128)} %bitcast.19, f32[32,16,256]{2,1,0:T(8,128)} %books_ref.1), custom_call_target="tpu_custom_call" | custom-call | tf_op jit(solution)/shard_map/pack/pallas_call | solution.py:92
  2.9 0.0 copy-start
  3.0 44.1 %all_to_all.21 = bf16[128,8,1152]{2,1,0:T(8,128)(2,1)S(1)} all-to-all(bf16[128,8,1152]{2,1,0:T(8,128)(2,1)S(1)} %bitcast.12), channel_id=1, replica_groups=mesh['far'=2,'plane'=16,'core'=2,'sub'=2] {'plane','core','far','sub'}, dimensions={0} | all-to-all | bytes 4718592 | tf_op jit(solution)/shard_map/all_to_all | solution.py:402
  47.1 0.0 copy-done
  47.1 11.1 %local_pass.1 = (f32[512,1024]{1,0:T(8,128)}, f32[1152,128]{1,0:T(8,128)S(1)}, f32[1152,128]{1,0:T(8,128)S(1)}) custom-call(s32[1]{0:T(128)} %bitcast.core_ref, bf16[1024,1152]{1,0:T(8,128)(2,1)S(1)} %bitcast.11, bf16[512,1024]{1,0:T(8,128)(2,1)S(1)} %copy-done), custom_call_target="tpu_custom_call" | custom-call | tf_op jit(solution)/shard_map/local_pass/pallas_call | solution.py:320
  58.2 0.1 collective-permute-start
  58.3 2.0 %collective-permute-done = f32[1152,128]{1,0:T(8,128)S(1)} collective-permute-done((f32[1152,128]{1,0:T(8,128)S(1)}, f32[1152,128]{1,0:T(8,128)S(1)}, u32[]{:S(2)}, u32[]{:S(2)}) %collective-permute-start) | collective-permute-done | bytes 589856 | tf_op jit(solution)/shard_map/ppermute | solution.py:406
  60.3 0.1 add.7
  60.4 17.4 %all_to_all.22 = f32[64,1,2304]{2,1,0:T(1,128)S(1)} all-to-all(f32[64,1,2304]{2,1,0:T(1,128)S(1)} %bitcast.17), channel_id=1, replica_groups=mesh['far'=2,'plane'=16,'core'=2,'sub'=2] {'sub','plane','far'}, dimensions={0} | all-to-all | bytes 1179648 | tf_op jit(solution)/shard_map/all_to_all | solution.py:408
  77.7 0.2 owner_pass.1
  77.9 11.6 %all_to_all.23 = f32[32,1,2176]{2,1,0:T(1,128)S(1)} all-to-all(f32[32,1,2176]{2,1,0:T(1,128)S(1)} %bitcast.16), channel_id=1, replica_groups=mesh['far'=2,'plane'=16,'core'=2,'sub'=2] {'far','plane'}, dimensions={0} | all-to-all | bytes 557056 | tf_op jit(solution)/shard_map/all_to_all | solution.py:424
  89.6 3.1 %collective-permute-start.1 = (f32[544,128]{1,0:T(8,128)S(1)}, f32[544,128]{1,0:T(8,128)S(1)}, u32[]{:S(2)}, u32[]{:S(2)}) collective-permute-start(f32[544,128]{1,0:T(8,128)S(1)} %bitcast.14), channel_id=1, source_target_pairs={{0,2},{2,0},{1,3},{3,1},{4,6},{6,4},{5,7},{7,5},{8,10},{10,8},{9,1... | collective-permute-start | bytes 835592 | tf_op jit(solution)/shard_map/ppermute | solution.py:427
  92.7 1.2 %collective-permute-done.1.other_ref = f32[544,128]{1,0:T(8,128)S(1)} collective-permute-done((f32[544,128]{1,0:T(8,128)S(1)}, f32[544,128]{1,0:T(8,128)S(1)}, u32[]{:S(2)}, u32[]{:S(2)}) %collective-permute-start.1) | collective-permute-done | bytes 278560 | tf_op jit(solution)/shard_map/ppermute | solution.py:427
  93.9 0.8 finish.1
Async XLA Ops:
  2.9 44.2 %copy-start = (bf16[512,1024]{1,0:T(8,128)(2,1)S(1)}, bf16[512,1024]{1,0:T(8,128)(2,1)}, u32[]{:S(2)}) copy-start(bf16[512,1024]{1,0:T(8,128)(2,1)} %cent_ref.1) | copy-start | bytes 3145732
  58.2 2.1 %collective-permute-start = (f32[1152,128]{1,0:T(8,128)S(1)}, f32[1152,128]{1,0:T(8,128)S(1)}, u32[]{:S(2)}, u32[]{:S(2)}) collective-permute-start(f32[1152,128]{1,0:T(8,128)S(1)} %get-tuple-element.13), channel_id=1, source_target_pairs={{0,2},{2,0},{1,3},{3,1},{4,6},{6,4},{5,7},{7,5},{8,10},{10,8},{9,1... | collective-permute-start | bytes 1769480 | tf_op jit(solution)/shard_map/ppermute | solution.py:406
  89.6 4.3 %collective-permute-start.1 = (f32[544,128]{1,0:T(8,128)S(1)}, f32[544,128]{1,0:T(8,128)S(1)}, u32[]{:S(2)}, u32[]{:S(2)}) collective-permute-start(f32[544,128]{1,0:T(8,128)S(1)} %bitcast.14), channel_id=1, source_target_pairs={{0,2},{2,0},{1,3},{3,1},{4,6},{6,4},{5,7},{7,5},{8,10},{10,8},{9,1... | collective-permute-start | bytes 835592 | tf_op jit(solution)/shard_map/ppermute | solution.py:427

commit v9 on v8

--- a/solution.py
+++ b/solution.py
@@ -13,10 +13,12 @@
 MIB = 1024 * 1024
 IN_VMEM = pl.BlockSpec(memory_space=pltpu.VMEM)
 FAR = 2
-SPLIT = ("far", "plane", "core", "sub")
-CHIP = ("far", "plane")
-ROW_ORDER = ("plane", "core", "far", "sub")
-SUM_ORDER = ("sub", "plane", "far")
+DEEP = 4
+SPLIT = ("far", "y", "z", "core", "sub")
+CHIP = ("far", "y", "z")
+ROW_ORDER = ("far", "z", "core", "y", "sub")
+SUM_ORDER = ("sub", "y", "z", "far")
+RESULT_ORDER = ("far", "z", "y")
 
 
 def split3(x):
@@ -32,27 +34,27 @@
 
 
 def pack_kernel(
-    lists, pieces, place, v_ref, ids_ref, codes_ref, books_ref, out_ref, old_ref, ids_v, codes_v, sems
+    lists, place, v_ref, ids_ref, codes_ref, books_ref, out_ref, old_ref, ids_v, codes_v, sems
 ):
-    far, runs, run, dims = v_ref.shape
+    far, deep, runs, run, dims = v_ref.shape
     subs, rows = codes_ref.shape
-    step = runs // pieces
+    pieces = far * deep
     half = pl.ds(pl.multiple_of(place[1] * LANES, LANES), LANES)
     small = [
-        pltpu.make_async_copy(codes_ref, codes_v, sems.at[far * pieces]),
-        pltpu.make_async_copy(ids_ref, ids_v, sems.at[far * pieces + 1]),
+        pltpu.make_async_copy(codes_ref, codes_v, sems.at[pieces]),
+        pltpu.make_async_copy(ids_ref, ids_v, sems.at[pieces + 1]),
     ]
     moves = [
         pltpu.make_async_copy(
-            v_ref.at[f, pl.ds(i * step, step)],
-            out_ref.at[pl.ds(i * step, step), f, :, pl.ds(0, dims)],
-            sems.at[f * pieces + i],
+            v_ref.at[f, y],
+            out_ref.at[f, :, y, :, pl.ds(0, dims)],
+            sems.at[f * deep + y],
         )
         for f in range(far)
-        for i in range(pieces)
+        for y in range(deep)
     ]
     moves.append(
-        pltpu.make_async_copy(books_ref.at[place[0], :, half], old_ref, sems.at[far * pieces + 2])
+        pltpu.make_async_copy(books_ref.at[place[0], :, half], old_ref, sems.at[pieces + 2])
     )
     for move in small + moves:
         move.start()
@@ -69,9 +71,10 @@
         ],
         axis=0,
     )
-    aux = jnp.transpose(aux).astype(jnp.bfloat16).reshape(far, runs, run, LANES)
+    aux = jnp.transpose(aux).astype(jnp.bfloat16).reshape(far, deep, runs, run, LANES)
     for f in range(far):
-        out_ref[:, f, :, dims:] = aux[f]
+        for y in range(deep):
+            out_ref[f, :, y, :, dims:] = aux[f, y]
     for move in moves:
         move.wait()
 
@@ -80,27 +83,26 @@
     rows, dims = vectors.shape
     subs = codes.shape[1]
     width = codebooks.shape[1]
-    pieces = 2
-    runs = rows // (FAR * run)
+    runs = rows // (FAR * DEEP * run)
     anywhere = pl.BlockSpec(memory_space=pl.ANY)
     sources = (
-        vectors.reshape(FAR, runs, run, dims),
+        vectors.reshape(FAR, DEEP, runs, run, dims),
         list_ids.reshape(1, rows),
         jnp.transpose(codes),
         codebooks,
     )
     sent, old = pl.pallas_call(
-        functools.partial(pack_kernel, lists, pieces),
+        functools.partial(pack_kernel, lists),
         in_specs=[pl.BlockSpec(memory_space=pltpu.SMEM)] + [anywhere] * 4,
         out_specs=[IN_VMEM, IN_VMEM],
         out_shape=[
-            jax.ShapeDtypeStruct((runs, FAR, run, dims + LANES), jnp.bfloat16),
+            jax.ShapeDtypeStruct((FAR, runs, DEEP, run, dims + LANES), jnp.bfloat16),
             jax.ShapeDtypeStruct((width, LANES), jnp.float32),
         ],
         scratch_shapes=[
             pltpu.VMEM((1, rows), jnp.int32),
             pltpu.VMEM((subs, rows), jnp.int32),
-            pltpu.SemaphoreType.DMA((FAR * pieces + 3,)),
+            pltpu.SemaphoreType.DMA((FAR * DEEP + 3,)),
         ],
         compiler_params=pltpu.CompilerParams(vmem_limit_bytes=12 * MIB),
         name="pack",
@@ -372,19 +374,27 @@
 def finish_kernel(width, core_ref, mine_ref, other_ref, table_ref, dist_ref):
     held = width + 1
     subs = table_ref.shape[0]
+    wide = subs // (FAR * DEEP)
     first_core = core_ref[0] == 0
-    for ref, at in ((0, slice(0, LANES)), (1, slice(LANES, 2 * LANES))):
-        own = first_core if ref == 0 else jnp.logical_not(first_core)
-        for m in range(subs):
-            rows = slice(m * held, m * held + width)
-            table_ref[m, :, at] = jnp.where(own, mine_ref[rows], other_ref[rows])
-        last = pl.ds(width, subs, stride=held)
-        dist_ref[:, at] = jnp.where(own, mine_ref[last, :], other_ref[last, :])
+    for half, at in ((0, slice(0, LANES)), (1, slice(LANES, 2 * LANES))):
+        own = first_core if half == 0 else jnp.logical_not(first_core)
+        for block in range(FAR * DEEP):
+            far, y = divmod(block, DEEP)
+            start = (far * wide * DEEP + y) * held
+            for z in range(wide):
+                rows = slice(start + z * DEEP * held, start + z * DEEP * held + width)
+                table_ref[block * wide + z, :, at] = jnp.where(
+                    own, mine_ref[rows], other_ref[rows]
+                )
+            last = pl.ds(start + width, wide, stride=DEEP * held)
+            dist_ref[block * wide : (block + 1) * wide, at] = jnp.where(
+                own, mine_ref[last, :], other_ref[last, :]
+            )
 
 
 def on_device(vectors, list_ids, codes, centroids, codebooks):
     rows, dims = vectors.shape
-    chips = lax.axis_size("far") * lax.axis_size("plane")
+    chips = lax.axis_size("far") * lax.axis_size("y") * lax.axis_size("z")
     parts = lax.axis_size("sub")
     owners = chips * CORES * parts
     lists = centroids.shape[0]
@@ -422,7 +432,7 @@
         name="owner_pass",
     )(mine, old)
     half = lax.all_to_all(
-        done.reshape(chips, 1, held * LANES), CHIP, split_axis=0, concat_axis=0, tiled=True
+        done.reshape(chips, 1, held * LANES), RESULT_ORDER, split_axis=0, concat_axis=0, tiled=True
     ).reshape(chips * held, LANES)
     other = lax.ppermute(half, "core", swap)
     table, distortion = pl.pallas_call(
@@ -441,7 +451,7 @@
 
 def solution(mesh):
     parts = mesh.shape["sub"]
-    cores = Mesh(mesh.devices.reshape(FAR, -1, CORES, parts), SPLIT)
+    cores = Mesh(mesh.devices.reshape(FAR, DEEP, -1, CORES, parts), SPLIT)
     in_specs = (
         P(SPLIT, None),
         P(SPLIT),

time: 95 us -> 94.7 us (level)
  starting transfers between devices: 3.23 us -> 4.76 us
  blocking collectives: 73.1 us -> 71.7 us
    ppermute x1, starting transfers between devices: 0.09 us -> 1.71 us  [on_device(): paired = keep + lax.ppermute(give, 'core', swap)]
    all_to_all x1, blocking collectives: 44.1 us -> 43.1 us  [on_device(): lax.all_to_all(sent, ROW_ORDER, split_axis=0, concat_axis=0, tiled=True)]
where the time goes in v9:
time: 94.7 us; the launch traced here: 94.5 us
  blocking collectives  71.7 us (76%)
  Pallas kernels  14.4 us (15%)
  starting transfers between devices  4.76 us (5%)
  waiting for transfers between devices  2.82 us (3%)
    all_to_all x1, blocking collectives, on_device(): lax.all_to_all(sent, ROW_ORDER, split_axis=0, concat_axis=0, tiled=True)  43.1 us
    all_to_all x1, blocking collectives, on_device(): lax.all_to_all(paired.reshape(chips * parts, 1, held * LANES), SUM_ORDER,...  17 us
    all_to_all x1, blocking collectives, on_device(): lax.all_to_all(done.reshape(chips, 1, held * LANES), RESULT_ORDER, split_...  11.7 us
    pallas_call x1, Pallas kernels, local_pass(): pl.pallas_call(functools.partial(local_kernel, subs, width, parts, prior,...  11.1 us
    ppermute x1, starting transfers between devices, on_device(): other = lax.ppermute(half, 'core', swap)  3.05 us
    pallas_call x1, Pallas kernels, pack(): pl.pallas_call(functools.partial(pack_kernel, lists), in_specs=[pl.BlockS...  2.24 us
  transfers between devices with their start and end apart: 2, of which 2 were waited for; matrix products, arithmetic and copies ran while one was open for 0% of the time, Pallas kernels for 0%

profile of v9, /device:TPU:1, one launch (start us, length us, event | category | flops | bytes accessed | tf_op | source)
XLA Modules:
  0.0 94.5 jit_solution(13268461064306769398)
XLA Ops:
  0.6 0.1 pad_add_fusion.place
  0.7 2.2 %pack.1 = (bf16[2,8,4,16,1152]{4,3,2,1,0:T(8,128)(2,1)S(1)}, f32[16,128]{1,0:T(8,128)S(1)}) custom-call(s32[2]{0:T(128)S(1)} %pad_add_fusion.place, bf16[2,4,8,16,1024]{4,3,2,1,0:T(8,128)(2,1)} %bitcast.18, s32[1,1024]{1,0:T(1,128)} %bitcast.20, s32[64,1024]{1,0:T(8,128)} %bitcast.19, f32[32,16,256]{2,1,0:T(8,128)} %books_ref.1), custom_call_target="tpu_custom_call" | custom-call | tf_op jit(solution)/shard_map/pack/pallas_call | solution.py:94
  3.0 0.0 copy-start
  3.0 43.1 %all_to_all.21 = bf16[128,8,1152]{2,1,0:T(8,128)(2,1)S(1)} all-to-all(bf16[128,8,1152]{2,1,0:T(8,128)(2,1)S(1)} %bitcast.12), channel_id=1, replica_groups=mesh['far'=2,'y'=4,'z'=4,'core'=2,'sub'=2] {'far','z','core','y','sub'}, dimensions={0} | all-to-all | bytes 4718592 | tf_op jit(solution)/shard_map/all_to_all | solution.py:412
  46.0 0.0 copy-done
  46.0 11.1 %local_pass.1 = (f32[512,1024]{1,0:T(8,128)}, f32[1152,128]{1,0:T(8,128)S(1)}, f32[1152,128]{1,0:T(8,128)S(1)}) custom-call(s32[1]{0:T(128)} %bitcast.core_ref, bf16[1024,1152]{1,0:T(8,128)(2,1)S(1)} %bitcast.11, bf16[512,1024]{1,0:T(8,128)(2,1)S(1)} %copy-done), custom_call_target="tpu_custom_call" | custom-call | tf_op jit(solution)/shard_map/local_pass/pallas_call | solution.py:322
  57.1 1.7 %collective-permute-start = (f32[1152,128]{1,0:T(8,128)S(1)}, f32[1152,128]{1,0:T(8,128)S(1)}, u32[]{:S(2)}, u32[]{:S(2)}) collective-permute-start(f32[1152,128]{1,0:T(8,128)S(1)} %get-tuple-element.13), channel_id=1, source_target_pairs={{0,2},{2,0},{1,3},{3,1},{4,6},{6,4},{5,7},{7,5},{8,10},{10,8},{9,1... | collective-permute-start | bytes 1769480 | tf_op jit(solution)/shard_map/ppermute | solution.py:416
  58.9 1.6 %collective-permute-done = f32[1152,128]{1,0:T(8,128)S(1)} collective-permute-done((f32[1152,128]{1,0:T(8,128)S(1)}, f32[1152,128]{1,0:T(8,128)S(1)}, u32[]{:S(2)}, u32[]{:S(2)}) %collective-permute-start) | collective-permute-done | bytes 589856 | tf_op jit(solution)/shard_map/ppermute | solution.py:416
  60.5 0.1 add.11
  60.6 17.0 %all_to_all.22 = f32[64,1,2304]{2,1,0:T(1,128)S(1)} all-to-all(f32[64,1,2304]{2,1,0:T(1,128)S(1)} %bitcast.17), channel_id=1, replica_groups=mesh['far'=2,'y'=4,'z'=4,'core'=2,'sub'=2] {'sub','y','z','far'}, dimensions={0} | all-to-all | bytes 1179648 | tf_op jit(solution)/shard_map/all_to_all | solution.py:418
  77.5 0.2 owner_pass.1
  77.7 11.7 %all_to_all.23 = f32[32,1,2176]{2,1,0:T(1,128)S(1)} all-to-all(f32[32,1,2176]{2,1,0:T(1,128)S(1)} %bitcast.16), channel_id=1, replica_groups=mesh['far'=2,'y'=4,'z'=4,'core'=2,'sub'=2] {'far','z','y'}, dimensions={0} | all-to-all | bytes 557056 | tf_op jit(solution)/shard_map/all_to_all | solution.py:434
  89.4 3.0 %collective-permute-start.1 = (f32[544,128]{1,0:T(8,128)S(1)}, f32[544,128]{1,0:T(8,128)S(1)}, u32[]{:S(2)}, u32[]{:S(2)}) collective-permute-start(f32[544,128]{1,0:T(8,128)S(1)} %bitcast.14), channel_id=1, source_target_pairs={{0,2},{2,0},{1,3},{3,1},{4,6},{6,4},{5,7},{7,5},{8,10},{10,8},{9,1... | collective-permute-start | bytes 835592 | tf_op jit(solution)/shard_map/ppermute | solution.py:437
  92.4 1.2 %collective-permute-done.1.other_ref = f32[544,128]{1,0:T(8,128)S(1)} collective-permute-done((f32[544,128]{1,0:T(8,128)S(1)}, f32[544,128]{1,0:T(8,128)S(1)}, u32[]{:S(2)}, u32[]{:S(2)}) %collective-permute-start.1) | collective-permute-done | bytes 278560 | tf_op jit(solution)/shard_map/ppermute | solution.py:437
  93.6 0.8 finish.1
Async XLA Ops:
  3.0 43.1 %copy-start = (bf16[512,1024]{1,0:T(8,128)(2,1)S(1)}, bf16[512,1024]{1,0:T(8,128)(2,1)}, u32[]{:S(2)}) copy-start(bf16[512,1024]{1,0:T(8,128)(2,1)} %cent_ref.1) | copy-start | bytes 3145732
  57.1 3.3 %collective-permute-start = (f32[1152,128]{1,0:T(8,128)S(1)}, f32[1152,128]{1,0:T(8,128)S(1)}, u32[]{:S(2)}, u32[]{:S(2)}) collective-permute-start(f32[1152,128]{1,0:T(8,128)S(1)} %get-tuple-element.13), channel_id=1, source_target_pairs={{0,2},{2,0},{1,3},{3,1},{4,6},{6,4},{5,7},{7,5},{8,10},{10,8},{9,1... | collective-permute-start | bytes 1769480 | tf_op jit(solution)/shard_map/ppermute | solution.py:416
  89.4 4.2 %collective-permute-start.1 = (f32[544,128]{1,0:T(8,128)S(1)}, f32[544,128]{1,0:T(8,128)S(1)}, u32[]{:S(2)}, u32[]{:S(2)}) collective-permute-start(f32[544,128]{1,0:T(8,128)S(1)} %bitcast.14), channel_id=1, source_target_pairs={{0,2},{2,0},{1,3},{3,1},{4,6},{6,4},{5,7},{7,5},{8,10},{10,8},{9,1... | collective-permute-start | bytes 835592 | tf_op jit(solution)/shard_map/ppermute | solution.py:437

commit v10 on v8

--- a/solution.py
+++ b/solution.py
@@ -369,17 +369,42 @@
         out_ref[c * (width + 1) : (c + 1) * (width + 1)] = result
 
 
-def finish_kernel(width, core_ref, mine_ref, other_ref, table_ref, dist_ref):
+def half_kernel(width, flip, core_ref, part_ref, *refs):
+    table_ref, dist_ref, table_v, dist_v, sems = refs[-5:]
     held = width + 1
     subs = table_ref.shape[0]
-    first_core = core_ref[0] == 0
-    for ref, at in ((0, slice(0, LANES)), (1, slice(LANES, 2 * LANES))):
-        own = first_core if ref == 0 else jnp.logical_not(first_core)
-        for m in range(subs):
-            rows = slice(m * held, m * held + width)
-            table_ref[m, :, at] = jnp.where(own, mine_ref[rows], other_ref[rows])
-        last = pl.ds(width, subs, stride=held)
-        dist_ref[:, at] = jnp.where(own, mine_ref[last, :], other_ref[last, :])
+    half = core_ref[0] if flip == 0 else 1 - core_ref[0]
+    at = pl.ds(pl.multiple_of(half * LANES, LANES), LANES)
+    dist_v[...] = part_ref[pl.ds(width, subs, stride=held), :]
+    dist_move = pltpu.make_async_copy(dist_v, dist_ref.at[:, at], sems.at[0])
+    dist_move.start()
+    for m in range(subs):
+        table_v[m] = part_ref[m * held : m * held + width]
+    table_move = pltpu.make_async_copy(table_v, table_ref.at[:, :, at], sems.at[1])
+    table_move.start()
+    dist_move.wait()
+    table_move.wait()
+
+
+def write_half(flip, core, part, shapes, held_before):
+    subs, width, _ = shapes[0].shape
+    anywhere = pl.BlockSpec(memory_space=pl.ANY)
+    return pl.pallas_call(
+        functools.partial(half_kernel, width, flip),
+        in_specs=[pl.BlockSpec(memory_space=pltpu.SMEM), IN_VMEM]
+        + [anywhere] * len(held_before),
+        out_specs=[anywhere, anywhere],
+        out_shape=list(shapes),
+        input_output_aliases={2: 0, 3: 1} if held_before else {},
+        scratch_shapes=[
+            pltpu.VMEM((subs, width, LANES), jnp.float32),
+            pltpu.VMEM((subs, LANES), jnp.float32),
+            pltpu.SemaphoreType.DMA((2,)),
+        ],
+        compiler_params=pltpu.CompilerParams(vmem_limit_bytes=8 * MIB),
+        cost_estimate=pl.CostEstimate(flops=0, bytes_accessed=4 * MIB, transcendentals=0),
+        name="own_half" if flip == 0 else "other_half",
+    )(core, part, *held_before)
 
 
 def on_device(vectors, list_ids, codes, centroids, codebooks):
@@ -425,17 +450,12 @@
         done.reshape(chips, 1, held * LANES), CHIP, split_axis=0, concat_axis=0, tiled=True
     ).reshape(chips * held, LANES)
     other = lax.ppermute(half, "core", swap)
-    table, distortion = pl.pallas_call(
-        functools.partial(finish_kernel, width),
-        in_specs=[pl.BlockSpec(memory_space=pltpu.SMEM), IN_VMEM, IN_VMEM],
-        out_specs=[IN_VMEM, IN_VMEM],
-        out_shape=[
-            jax.ShapeDtypeStruct((my_subs, width, levels), jnp.float32),
-            jax.ShapeDtypeStruct((my_subs, levels), jnp.float32),
-        ],
-        compiler_params=pltpu.CompilerParams(vmem_limit_bytes=8 * MIB),
-        name="finish",
-    )(core_arg, half, other)
+    shapes = (
+        jax.ShapeDtypeStruct((my_subs, width, levels), jnp.float32),
+        jax.ShapeDtypeStruct((my_subs, levels), jnp.float32),
+    )
+    first = write_half(0, core_arg, half, shapes, ())
+    table, distortion = write_half(1, core_arg, other, shapes, tuple(first))
     return new_centroids, table, distortion
 
 

time: 95 us -> 94.9 us (level)
  transfers between devices with their start and end apart: 2 -> 2, of which waited for: 2 -> 2; matrix products, arithmetic and copies ran while one was open for 0% -> 0% of each run, Pallas kernels for 0% -> 1%
where the time goes in v10:
time: 94.9 us; the launch traced here: 94.6 us
  blocking collectives  73.1 us (77%)
  Pallas kernels  15 us (16%)
  starting transfers between devices  3.23 us (3%)
  waiting for transfers between devices  2.43 us (3%)
    all_to_all x1, blocking collectives, on_device(): lax.all_to_all(sent, ROW_ORDER, split_axis=0, concat_axis=0, tiled=True)  44.1 us
    all_to_all x1, blocking collectives, on_device(): lax.all_to_all(paired.reshape(chips * parts, 1, held * LANES), SUM_ORDER,...  17.4 us
    all_to_all x1, blocking collectives, on_device(): lax.all_to_all(done.reshape(chips, 1, held * LANES), CHIP, split_axis=0,...  11.6 us
    pallas_call x1, Pallas kernels, local_pass(): pl.pallas_call(functools.partial(local_kernel, subs, width, parts, prior,...  11.1 us
    ppermute x1, starting transfers between devices, on_device(): other = lax.ppermute(half, 'core', swap)  3.15 us
    pallas_call x1, Pallas kernels, pack(): pl.pallas_call(functools.partial(pack_kernel, lists, pieces), in_specs=[p...  2.22 us
    ppermute x1, waiting for transfers between devices, on_device(): paired = keep + lax.ppermute(give, 'core', swap)  1.99 us
  transfers between devices with their start and end apart: 2, of which 2 were waited for; matrix products, arithmetic and copies ran while one was open for 0% of the time, Pallas kernels for 1%

profile of v10, /device:TPU:1, one launch (start us, length us, event | category | flops | bytes accessed | tf_op | source)
XLA Modules:
  0.0 94.6 jit_solution(9619207636833498734)
XLA Ops:
  0.6 0.1 pad_add_fusion.place
  0.7 2.2 %pack.1 = (bf16[32,2,16,1152]{3,2,1,0:T(8,128)(2,1)S(1)}, f32[16,128]{1,0:T(8,128)S(1)}) custom-call(s32[2]{0:T(128)S(1)} %pad_add_fusion.place, bf16[2,32,16,1024]{3,2,1,0:T(8,128)(2,1)} %bitcast.18, s32[1,1024]{1,0:T(1,128)} %bitcast.20, s32[64,1024]{1,0:T(8,128)} %bitcast.19, f32[32,16,256]{2,1,0:T(8,128)} %books_ref.1), custom_call_target="tpu_custom_call" | custom-call | tf_op jit(solution)/shard_map/pack/pallas_call | solution.py:92
  2.9 0.0 copy-start
  3.0 44.1 %all_to_all.21 = bf16[128,8,1152]{2,1,0:T(8,128)(2,1)S(1)} all-to-all(bf16[128,8,1152]{2,1,0:T(8,128)(2,1)S(1)} %bitcast.12), channel_id=1, replica_groups=mesh['far'=2,'plane'=16,'core'=2,'sub'=2] {'plane','core','far','sub'}, dimensions={0} | all-to-all | bytes 4718592 | tf_op jit(solution)/shard_map/all_to_all | solution.py:427
  47.1 0.0 copy-done
  47.1 11.1 %local_pass.1 = (f32[512,1024]{1,0:T(8,128)}, f32[1152,128]{1,0:T(8,128)S(1)}, f32[1152,128]{1,0:T(8,128)S(1)}) custom-call(s32[1]{0:T(128)} %bitcast.core_ref, bf16[1024,1152]{1,0:T(8,128)(2,1)S(1)} %bitcast.11, bf16[512,1024]{1,0:T(8,128)(2,1)S(1)} %copy-done), custom_call_target="tpu_custom_call" | custom-call | tf_op jit(solution)/shard_map/local_pass/pallas_call | solution.py:320
  58.2 0.1 collective-permute-start
  58.3 2.0 %collective-permute-done = f32[1152,128]{1,0:T(8,128)S(1)} collective-permute-done((f32[1152,128]{1,0:T(8,128)S(1)}, f32[1152,128]{1,0:T(8,128)S(1)}, u32[]{:S(2)}, u32[]{:S(2)}) %collective-permute-start) | collective-permute-done | bytes 589856 | tf_op jit(solution)/shard_map/ppermute | solution.py:431
  60.3 0.1 add.7
  60.4 17.4 %all_to_all.22 = f32[64,1,2304]{2,1,0:T(1,128)S(1)} all-to-all(f32[64,1,2304]{2,1,0:T(1,128)S(1)} %bitcast.17), channel_id=1, replica_groups=mesh['far'=2,'plane'=16,'core'=2,'sub'=2] {'sub','plane','far'}, dimensions={0} | all-to-all | bytes 1179648 | tf_op jit(solution)/shard_map/all_to_all | solution.py:433
  77.7 0.2 owner_pass.1
  77.9 11.6 %all_to_all.23 = f32[32,1,2176]{2,1,0:T(1,128)S(1)} all-to-all(f32[32,1,2176]{2,1,0:T(1,128)S(1)} %bitcast.16), channel_id=1, replica_groups=mesh['far'=2,'plane'=16,'core'=2,'sub'=2] {'far','plane'}, dimensions={0} | all-to-all | bytes 557056 | tf_op jit(solution)/shard_map/all_to_all | solution.py:449
  89.6 3.1 %collective-permute-start.1 = (f32[544,128]{1,0:T(8,128)S(1)}, f32[544,128]{1,0:T(8,128)S(1)}, u32[]{:S(2)}, u32[]{:S(2)}) collective-permute-start(f32[544,128]{1,0:T(8,128)S(1)} %bitcast.14), channel_id=1, source_target_pairs={{0,2},{2,0},{1,3},{3,1},{4,6},{6,4},{5,7},{7,5},{8,10},{10,8},{9,1... | collective-permute-start | bytes 835592 | tf_op jit(solution)/shard_map/ppermute | solution.py:452
  92.7 0.7 own_half.1
  93.5 0.4 collective-permute-done.1.part_ref
  93.9 0.7 other_half.1
Async XLA Ops:
  2.9 44.2 %copy-start = (bf16[512,1024]{1,0:T(8,128)(2,1)S(1)}, bf16[512,1024]{1,0:T(8,128)(2,1)}, u32[]{:S(2)}) copy-start(bf16[512,1024]{1,0:T(8,128)(2,1)} %cent_ref.1) | copy-start | bytes 3145732
  58.2 2.1 %collective-permute-start = (f32[1152,128]{1,0:T(8,128)S(1)}, f32[1152,128]{1,0:T(8,128)S(1)}, u32[]{:S(2)}, u32[]{:S(2)}) collective-permute-start(f32[1152,128]{1,0:T(8,128)S(1)} %get-tuple-element.15), channel_id=1, source_target_pairs={{0,2},{2,0},{1,3},{3,1},{4,6},{6,4},{5,7},{7,5},{8,10},{10,8},{9,1... | collective-permute-start | bytes 1769480 | tf_op jit(solution)/shard_map/ppermute | solution.py:431
  89.6 4.3 %collective-permute-start.1 = (f32[544,128]{1,0:T(8,128)S(1)}, f32[544,128]{1,0:T(8,128)S(1)}, u32[]{:S(2)}, u32[]{:S(2)}) collective-permute-start(f32[544,128]{1,0:T(8,128)S(1)} %bitcast.14), channel_id=1, source_target_pairs={{0,2},{2,0},{1,3},{3,1},{4,6},{6,4},{5,7},{7,5},{8,10},{10,8},{9,1... | collective-permute-start | bytes 835592 | tf_op jit(solution)/shard_map/ppermute | solution.py:452
